TPU v7x, 256 devices: a whole 4x4x8 slice. The times are simulated.
256 devices in a mesh: dom: 256 (over z, y, x, core).
Axes of the slice: x: 4, y: 4, z: 8, core: 2. Of those that a mesh axis runs over, the one named last changes fastest.
Arguments:
- fwd_dofs: float32 [35, 9, 65536], P(None, None, 'dom'), may hold values from -6 to 6
- adj_dofs: float32 [35, 9, 65536], P(None, None, 'dom'), may hold values from -6 to 6
- star: float32 [3, 9, 9, 65536], P(None, None, None, 'dom'), may hold values from -4 to 4
- flux_local: float32 [4, 9, 9, 65536], P(None, None, None, 'dom'), may hold values from -2 to 2
- flux_neighbor: float32 [4, 9, 9, 65536], P(None, None, None, 'dom'), may hold values from -2 to 2
- timescale: float32 [65536], P('dom'), may hold values from 0.6 to 4.05
- cluster: int32 [65536], P('dom'), may hold values from 0 to 3, as said below
- face_kind: int32 [4, 65536], P(None, 'dom'), may hold values from 0 to 3, as said below
- neighbor_index: int32 [4, 65536], P(None, 'dom'), may hold values from 0 to 255, as said below
- neighbor_face: int32 [4, 65536], P(None, 'dom'), may hold values from 0 to 3, as said below
- orientation: int32 [4, 65536], P(None, 'dom'), may hold values from 0 to 2
- send_element: int32 [4, 16384], P(None, 'dom'), may hold values from 0 to 255, as said below
- send_face: int32 [4, 16384], P(None, 'dom'), may hold values from 0 to 3, as said below
- stiffness: float32 [3, 35, 35], replicated, may hold values from -1 to 1
- face_proj: float32 [4, 15, 35], replicated, may hold values from -1 to 1
- face_lift: float32 [4, 35, 15], replicated, may hold values from -1.5 to 1.5
- face_orient: float32 [3, 15, 15], replicated, may hold values from -1.5 to 1.5
Outputs:
- fwd_final: float32 [35, 9, 65536], P(None, None, 'dom')
- adj_final: float32 [35, 9, 65536], P(None, None, 'dom')
- sensitivity: float32 [65536], P('dom')
Inputs may be any that keep to these rules, and one draw needn't show every extreme that they name: At most 64 elements of one partition (one block of 256 consecutive entries) are in cluster 0, and some partition has exactly 64. `face_kind`: 0: neighbour in the same partition; 1: neighbour in another partition; 2: free surface; 3: absorbing boundary. A partition has exactly 64 faces of kind 1 toward each partition whose index differs by 1 or 2, when it exists. `neighbor_index`: kind 0: the neighbour's element in the partition, and that face names this element and face back. Kind 1: a receive slot g * 64 + j, the partition at index offset (-2, -1, 1, 2)[g] exists, and every such slot is named by exactly one face. Unused for kinds 2 and 3. `neighbor_face`: for kind 1 it equals the send_face entry of the slot that the face names. `send_element`: group g of a partition holds, slot by slot, its elements whose data go to the partition at index offset (2, 1, -1, -2)[g]; that partition names slot j of group g in its neighbor_index. Entries toward missing partitions are unused. `send_face`: the face of each send slot; the pair of element and face shares that face with the receiving element.
All inputs are finite; a program needn't handle non-finite values.
Results may differ from a plain program's by a relative error of at most 0.0003.
Values sent between devices are 32-bit elements; how exact they have to be, the bound alone decides.
No kernel may reach another device: no remote copies, remote signals or barrier semaphores. Data moves between devices by JAX's collectives and lax.ppermute only.
A program may use at most 128 MiB of HBM per device.

v0:
```python
import math

import jax
import jax.numpy as jnp
from jax import lax
from jax.experimental import pallas as pl
from jax.experimental.pallas import tpu as pltpu
from jax.sharding import PartitionSpec as P

BASIS = 35
FACE_BASIS = 15
QUANT = 9
ORDER = 5
ROWS = 40
PACK = 48
FROWS = 16
ELEMS = 256
SLOTS = 64
HALF = 128
TABLE = QUANT * FROWS
MIRRORED = (0, 3, 5)
F32 = jnp.float32
BF16 = jnp.bfloat16
VMEM_LIMIT = 16 * 1024 * 1024


def dot(a, b):
    return jnp.dot(a, b, preferred_element_type=F32)


def split(x):
    hi = x.astype(BF16)
    return hi, (x - hi.astype(F32)).astype(BF16)


def place(mat, cols, hi_at, lo_at):
    rows = mat.shape[1]
    gap = lax.broadcasted_iota(jnp.int32, (rows, cols), 1) - lax.broadcasted_iota(
        jnp.int32, (rows, cols), 0
    )

    def ones(starts):
        mask = gap == starts[0]
        for start in starts[1:]:
            mask = mask | (gap == start)
        return jnp.where(mask, 1.0, 0.0).astype(BF16)

    hi, lo = split(mat)
    return dot(hi, ones(hi_at)) + dot(lo, ones(lo_at))


def fill_stiff(out, stage, stiffness, transposed):
    stage[...] = jnp.zeros(stage.shape, F32)
    for d in range(3):
        mat = stiffness[d]
        if transposed:
            mat = mat.T
        stage[d * ROWS : d * ROWS + BASIS, 0 : 3 * PACK] = place(
            mat, 3 * PACK, (0, PACK), (2 * PACK,)
        )
    out[...] = stage[0 : 3 * ROWS, 0 : 3 * PACK].astype(BF16)


def fill_proj(out, stage, face_proj):
    stage[...] = jnp.zeros(stage.shape, F32)
    for f in range(4):
        stage[f * FROWS : f * FROWS + FACE_BASIS, 0 : 3 * PACK] = place(
            face_proj[:, f, :], 3 * PACK, (0, PACK), (2 * PACK,)
        )
    out[...] = stage[0 : 4 * FROWS, 0 : 3 * PACK].astype(BF16)


def fill_orient(out, stage, face_orient):
    stage[...] = jnp.zeros(stage.shape, F32)
    for o in range(3):
        stage[o * FROWS : o * FROWS + FACE_BASIS, 0 : 3 * FROWS] = place(
            face_orient[o], 3 * FROWS, (0, FROWS), (2 * FROWS,)
        )
    out[...] = stage[0 : 3 * FROWS, 0 : 3 * FROWS].astype(BF16)


def fill_lift(out, stage, face_lift):
    stage[...] = jnp.zeros(stage.shape, F32)
    total = jnp.zeros((BASIS, 12 * FROWS), F32)
    for f in range(4):
        base = f * FROWS
        total = total + place(
            face_lift[:, f, :].T, 12 * FROWS, (base, 4 * FROWS + base), (8 * FROWS + base,)
        )
    stage[0:BASIS, 0 : 12 * FROWS] = total
    out[...] = stage[0:ROWS, 0 : 12 * FROWS].astype(BF16)


def stack_split(x3, q, x):
    hi, lo = split(jnp.concatenate([x, jnp.zeros((PACK - ROWS, x.shape[1]), F32)], 0))
    x3[q, 0:PACK, :] = hi
    x3[q, PACK : 2 * PACK, :] = lo
    x3[q, 2 * PACK : 3 * PACK, :] = hi


def star_apply(spread, star, adjoint, half, emit):
    lanes = slice(half * HALF, half * HALF + HALF)
    acc = [None] * QUANT
    for p in range(QUANT):
        for d in range(3):
            value = spread[p, d * ROWS : d * ROWS + ROWS, lanes]
            for q in range(QUANT):
                if adjoint:
                    weight = star[p, q, d : d + 1, lanes]
                else:
                    weight = star[q, p, d : d + 1, lanes]
                term = value * weight
                acc[q] = term if acc[q] is None else acc[q] + term
    for q in range(QUANT):
        emit(q, lanes, acc[q])


def project(x3, wproj, table, n, faces=None):
    for q in range(QUANT):
        value = dot(wproj[...], x3[q])
        if faces is not None:
            faces[n, q] = value
        hi, lo = split(value)
        for f in range(4):
            lanes = slice(f * ELEMS, f * ELEMS + ELEMS)
            rows = slice(f * FROWS, f * FROWS + FROWS)
            base = n * 2 * TABLE + q * FROWS
            table[base : base + FROWS, lanes] = hi[rows]
            table[base + TABLE : base + TABLE + FROWS, lanes] = lo[rows]


def pack_send(table, pick, emit):
    found = dot(table[...], pick[...])
    low = lax.broadcasted_iota(jnp.int32, (TABLE, HALF), 1) < SLOTS
    sides = [
        found[n * 2 * TABLE : n * 2 * TABLE + TABLE]
        + found[n * 2 * TABLE + TABLE : n * 2 * TABLE + 2 * TABLE]
        for n in range(2)
    ]
    for pair in range(2):
        lanes = slice(pair * HALF, pair * HALF + HALF)
        first = sides[0][:, lanes]
        second = sides[1][:, lanes]
        emit(2 * pair, jnp.where(low, first, pltpu.roll(second, SLOTS, 1)))
        emit(2 * pair + 1, jnp.where(low, pltpu.roll(first, SLOTS, 1), second))


def unpack_received(groups, table):
    low = lax.broadcasted_iota(jnp.int32, (TABLE, HALF), 1) < SLOTS
    for pair in range(2):
        lanes = slice(pair * HALF, pair * HALF + HALF)
        first = groups[2 * pair]
        second = groups[2 * pair + 1]
        for n, value in enumerate(
            (
                jnp.where(low, first, pltpu.roll(second, SLOTS, 1)),
                jnp.where(low, pltpu.roll(first, SLOTS, 1), second),
            )
        ):
            hi, lo = split(value)
            table[n * 2 * TABLE : n * 2 * TABLE + TABLE, lanes] = hi
            table[n * 2 * TABLE + TABLE : n * 2 * TABLE + 2 * TABLE, lanes] = lo


def one_hot(codes, first, rows):
    ids = lax.broadcasted_iota(jnp.int32, (rows, codes.shape[1]), 0) + first
    return jnp.where(ids == codes, 1.0, 0.0).astype(BF16)


def first_kernel(
    fwd,
    adj,
    star,
    stiffness,
    face_proj,
    send_element,
    send_face,
    face_kind,
    neighbor_index,
    neighbor_face,
    cluster,
    orientation,
    face_lift,
    face_orient,
    flux_local,
    flux_neighbor,
    derived,
    pick_local,
    pick_remote,
    pick_send,
    pick_fine,
    fine_star,
    wstiff,
    wstiff_t,
    wproj,
    wlift,
    worient,
    star_kept,
    local_kept,
    neighbor_kept,
    kind_kept,
    turn_kept,
    cluster_kept,
    stage,
    x3,
    spread,
    codes,
    series,
    sems,
):
    copies = [
        pltpu.make_async_copy(source, kept, sems.at[ORDER - 1 + i])
        for i, (source, kept) in enumerate(
            ((star, star_kept), (flux_local, local_kept), (flux_neighbor, neighbor_kept))
        )
    ]
    for copy in copies:
        copy.start()
    star = star_kept
    kind_kept[...] = face_kind[...]
    turn_kept[...] = orientation[...]
    cluster_kept[...] = cluster[...]
    fill_stiff(wstiff, stage, stiffness, False)
    fill_stiff(wstiff_t, stage, stiffness, True)
    fill_proj(wproj, stage, face_proj)
    fill_lift(wlift, stage, face_lift)
    fill_orient(worient, stage, face_orient)

    for n, field in enumerate((fwd, adj)):
        for q in range(QUANT):
            series[0, n, q, 0:BASIS, :] = field[q]
            series[0, n, q, BASIS:ROWS, :] = jnp.zeros((ROWS - BASIS, ELEMS), F32)

    send_code = send_face[...] * ELEMS + send_element[...]
    for g in range(4):
        codes[0:1, g * SLOTS : g * SLOTS + SLOTS] = send_code[g : g + 1]
    for block in range(4):
        rows = slice(block * ELEMS, block * ELEMS + ELEMS)
        pick_send[rows, :] = one_hot(codes[0:1, :], block * ELEMS, ELEMS)
    for f in range(4):
        lanes = slice(f * ELEMS, f * ELEMS + ELEMS)
        kind = face_kind[f : f + 1, :]
        index = neighbor_index[f : f + 1, :]
        local = jnp.where(kind == 0, neighbor_face[f : f + 1, :] * ELEMS + index, -1)
        remote = jnp.where(kind == 1, index, -1)
        for block in range(4):
            rows = slice(block * ELEMS, block * ELEMS + ELEMS)
            pick_local[rows, lanes] = one_hot(local, block * ELEMS, ELEMS)
        pick_remote[:, lanes] = one_hot(remote, 0, ELEMS)

    fine = cluster[...] == 0
    upper = lax.broadcasted_iota(jnp.int32, (ELEMS, ELEMS), 0) < lax.broadcasted_iota(
        jnp.int32, (ELEMS, ELEMS), 1
    )
    flags = jnp.broadcast_to(jnp.where(fine, 1.0, 0.0), (FROWS, ELEMS)).astype(BF16)
    rank = dot(flags, jnp.where(upper, 1.0, 0.0).astype(BF16))[0:1]
    place_of = jnp.where(fine, rank.astype(jnp.int32), -1)
    slot = lax.broadcasted_iota(jnp.int32, (HALF, ELEMS), 0)
    slot = jnp.where(slot < SLOTS, slot, slot - SLOTS)
    chosen = jnp.where(slot == place_of, 1.0, 0.0)
    pick_fine[...] = chosen.astype(BF16)
    pick_t = chosen.T.astype(BF16)
    low1 = lax.broadcasted_iota(jnp.int32, (1, HALF), 1) < SLOTS
    copies[0].wait()
    for d in range(3):
        plain = []
        for q in range(QUANT):
            hi, lo = split(star[q, :, d, :])
            plain.append(dot(hi, pick_t) + dot(lo, pick_t))
        for q in range(QUANT):
            for p in range(QUANT):
                fine_star[q, p, d : d + 1, :] = jnp.where(
                    low1, plain[q][p : p + 1], plain[p][q : q + 1]
                )

    def step(degree, _):
        for n in range(2):
            for q in range(QUANT):
                stack_split(x3, q, series[degree, n, q])
            for q in range(QUANT):
                spread[q] = dot(wstiff[...], x3[q])
            for half in range(2):

                def emit(q, lanes, value):
                    series[degree + 1, n, q, :, lanes] = value

                star_apply(spread, star, n == 1, half, emit)
        pltpu.make_async_copy(series.at[degree + 1], derived.at[degree], sems.at[degree]).start()
        return 0

    lax.fori_loop(0, ORDER - 1, step, 0)
    copies[1].wait()
    copies[2].wait()
    for degree in range(ORDER - 1):
        pltpu.make_async_copy(series.at[degree + 1], derived.at[degree], sems.at[degree]).wait()


def weights_of(steps):
    dt = 0.5 * jnp.min(steps[...])
    early = []
    late = []
    power = dt
    for degree in range(ORDER):
        scale = 1.0 / math.factorial(degree + 1)
        early.append(power * scale)
        late.append(power * (scale * (2.0 ** (degree + 1) - 1.0)))
        power = power * dt
    return early, late


def integral_kernel(
    steps,
    fwd,
    adj,
    derived,
    pick_send,
    wproj,
    out0,
    out1,
    out2,
    out3,
    integral,
    later,
    faces,
    table,
    x3,
    series,
    sems,
):
    outs = (out0, out1, out2, out3)
    copies = [
        pltpu.make_async_copy(derived.at[degree], series.at[degree], sems.at[degree])
        for degree in range(ORDER - 1)
    ]
    for copy in copies:
        copy.start()
    early, late = weights_of(steps)
    for n, field in enumerate((fwd, adj)):
        for q in range(QUANT):
            for sums, weight in ((integral, early[0]), (later, late[0])):
                sums[n, q, 0:BASIS, :] = weight * field[q]
                sums[n, q, BASIS:ROWS, :] = jnp.zeros((ROWS - BASIS, ELEMS), F32)
    for copy in copies:
        copy.wait()
    for n in range(2):
        for q in range(QUANT):
            total = integral[n, q]
            after = later[n, q]
            for degree in range(1, ORDER):
                value = series[degree - 1, n, q]
                total = total + early[degree] * value
                after = after + late[degree] * value
            integral[n, q] = total
            later[n, q] = after
            stack_split(x3.at[n], q, total)
        project(x3.at[n], wproj, table, n, faces)

    def send(g, value):
        outs[g][...] = value

    pack_send(table, pick_send, send)


def flux_apply(source, weights, adjoint, n, f, half, acc):
    lanes = slice(half * HALF, half * HALF + HALF)
    rows = slice(f * FROWS, f * FROWS + FROWS)
    for p in range(QUANT):
        value = source[n, p, rows, lanes]
        for q in range(QUANT):
            if adjoint:
                weight = weights[p, q, f : f + 1, lanes]
            else:
                weight = weights[q, p, f : f + 1, lanes]
            term = value * weight
            acc[q] = term if acc[q] is None else acc[q] + term
    return acc


def local_part(
    x3, wstiff_t, spread, star, faces, table, flux_local, pick_local, volume, flux_sum, gathered
):
    for n in range(2):
        for q in range(QUANT):
            spread[q] = dot(wstiff_t[...], x3[n, q])
        for half in range(2):

            def emit(q, lanes, value):
                volume[n, q, :, lanes] = value

            star_apply(spread, star, n == 1, half, emit)
    for f in range(4):
        lanes = slice(f * ELEMS, f * ELEMS + ELEMS)
        found = dot(table[...], pick_local[:, lanes])
        for n in range(2):
            gathered[n, f] = (
                found[n * 2 * TABLE : n * 2 * TABLE + TABLE]
                + found[n * 2 * TABLE + TABLE : n * 2 * TABLE + 2 * TABLE]
            )
    for n in range(2):
        for f in range(4):
            for half in range(2):
                acc = flux_apply(faces, flux_local, n == 1, n, f, half, [None] * QUANT)
                for q in range(QUANT):
                    flux_sum[
                        n,
                        q,
                        f * FROWS : f * FROWS + FROWS,
                        half * HALF : half * HALF + HALF,
                    ] = acc[q]


def remote_part(
    groups,
    rtable,
    pick_remote,
    gathered,
    faces,
    face_kind,
    orientation,
    worient,
    x3o,
    other,
    flux_sum,
    flux_neighbor,
    x3l,
    wlift,
    volume,
    emit,
):
    unpack_received(groups, rtable)
    for f in range(4):
        lanes = slice(f * ELEMS, f * ELEMS + ELEMS)
        rows = slice(f * FROWS, f * FROWS + FROWS)
        found = dot(rtable[...], pick_remote[:, lanes])
        turn = orientation[f : f + 1, :]
        surface = face_kind[f : f + 1, :] == 2
        for n in range(2):
            total = (
                found[n * 2 * TABLE : n * 2 * TABLE + TABLE]
                + found[n * 2 * TABLE + TABLE : n * 2 * TABLE + 2 * TABLE]
                + gathered[n, f]
            )
            hi, lo = split(total)
            for q in range(QUANT):
                part = slice(q * FROWS, q * FROWS + FROWS)
                x3o[n, f, q, 0:FROWS, :] = hi[part]
                x3o[n, f, q, FROWS : 2 * FROWS, :] = lo[part]
                x3o[n, f, q, 2 * FROWS : 3 * FROWS, :] = hi[part]
            for q in range(QUANT):
                three = dot(worient[...], x3o[n, f, q])
                turned = jnp.where(
                    turn == 0,
                    three[0:FROWS],
                    jnp.where(turn == 1, three[FROWS : 2 * FROWS], three[2 * FROWS : 3 * FROWS]),
                )
                own = faces[n, q, rows, :]
                if q in MIRRORED:
                    own = -own
                other[n, q, rows, :] = turned + jnp.where(surface, own, 0.0)
    for n in range(2):
        for f in range(4):
            rows = slice(f * FROWS, f * FROWS + FROWS)
            for half in range(2):
                lanes = slice(half * HALF, half * HALF + HALF)
                acc = [flux_sum[n, q, rows, lanes] for q in range(QUANT)]
                acc = flux_apply(other, flux_neighbor, n == 1, n, f, half, acc)
                for q in range(QUANT):
                    hi, lo = split(acc[q])
                    x3l[q, f * FROWS : f * FROWS + FROWS, lanes] = hi
                    x3l[q, (4 + f) * FROWS : (5 + f) * FROWS, lanes] = lo
                    x3l[q, (8 + f) * FROWS : (9 + f) * FROWS, lanes] = hi
        for q in range(QUANT):
            emit(n, q, volume[n, q] + dot(wlift[...], x3l[q]))


def middle_kernel(
    steps,
    fwd,
    adj,
    integral,
    later,
    in0,
    in1,
    in2,
    in3,
    pick_remote,
    pick_send,
    pick_fine,
    fine_star,
    gathered,
    faces,
    face_kind,
    orientation,
    worient,
    flux_sum,
    flux_neighbor,
    wlift,
    volume,
    cluster,
    wstiff,
    wproj,
    out0,
    out1,
    out2,
    out3,
    base,
    faces_out,
    table,
    x3,
    sens,
    rtable,
    x3o,
    other,
    x3l,
    wide,
    x3c,
    spread_c,
    fields_c,
):
    outs = (out0, out1, out2, out3)
    early, _ = weights_of(steps)
    fine = cluster[...] == 0
    active = cluster[...] <= 1

    def emit_first(n, q, value):
        start = jnp.concatenate([(fwd, adj)[n][q], jnp.zeros((ROWS - BASIS, ELEMS), F32)], 0)
        moved = start + value
        base[n, q] = jnp.where(active, moved, start)
        hi, lo = split(moved)
        wide[q, 0:ROWS, 2 * n * ELEMS : (2 * n + 1) * ELEMS] = hi
        wide[q, 0:ROWS, (2 * n + 1) * ELEMS : (2 * n + 2) * ELEMS] = lo

    wide[...] = jnp.zeros(wide.shape, BF16)
    remote_part(
        [in0[...], in1[...], in2[...], in3[...]],
        rtable,
        pick_remote,
        gathered,
        faces,
        face_kind,
        orientation,
        worient,
        x3o,
        other,
        flux_sum,
        flux_neighbor,
        x3l,
        wlift,
        volume,
        emit_first,
    )

    slot = lax.broadcasted_iota(jnp.int32, (HALF, ELEMS), 0)
    chosen = pick_fine[...].astype(F32)
    mine = [jnp.where(slot < SLOTS, chosen, 0.0), jnp.where(slot < SLOTS, 0.0, chosen)]
    pick_t = [m.T.astype(BF16) for m in mine]
    mine = [m.astype(BF16) for m in mine]
    for q in range(QUANT):
        value = jnp.zeros((ROWS, HALF), F32)
        for n in range(2):
            for part in range(2):
                lanes = slice((2 * n + part) * ELEMS, (2 * n + part + 1) * ELEMS)
                value = value + dot(wide[q, :, lanes], pick_t[n])[0:ROWS]
        fields_c[q] = early[0] * value
        stack_split(x3c, q, value)
    for degree in range(1, ORDER):
        for q in range(QUANT):
            spread_c[q] = dot(wstiff[...], x3c[q])

        def emit(q, lanes, value):
            fields_c[q] = fields_c[q] + early[degree] * value
            if degree < ORDER - 1:
                stack_split(x3c, q, value)

        star_apply(spread_c, fine_star, False, 0, emit)

    products = jnp.zeros((ROWS, ELEMS), F32)
    for q in range(QUANT):
        hi, lo = split(jnp.concatenate([fields_c[q], jnp.zeros((PACK - ROWS, HALF), F32)], 0))
        both = []
        for n in range(2):
            renewed = (dot(hi, mine[n]) + dot(lo, mine[n]))[0:ROWS]
            value = jnp.where(fine, renewed, later[n, q])
            stack_split(x3.at[n], q, value)
            both.append(value)
        products = products + integral[0, q] * integral[1, q] + both[0] * both[1]
    sens[...] = jnp.sum(products, axis=0, keepdims=True)
    for n in range(2):
        project(x3.at[n], wproj, table, n, faces_out)

    def send(g, value):
        outs[g][...] = value

    pack_send(table, pick_send, send)


def local_kernel(
    x3, star, faces, table, flux_local, pick_local, wstiff_t, volume, flux_sum, gathered, spread
):
    local_part(
        x3, wstiff_t, spread, star, faces, table, flux_local, pick_local, volume, flux_sum, gathered
    )


def last_kernel(
    in0,
    in1,
    in2,
    in3,
    pick_remote,
    gathered,
    faces,
    face_kind,
    orientation,
    worient,
    flux_sum,
    flux_neighbor,
    wlift,
    volume,
    base,
    cluster,
    fwd,
    adj,
    rtable,
    x3o,
    other,
    x3l,
):
    active = cluster[...] <= 1
    outs = (fwd, adj)

    def emit(n, q, value):
        final = base[n, q] + jnp.where(active, value, 0.0)
        outs[n][q] = final[0:BASIS]

    remote_part(
        [in0[...], in1[...], in2[...], in3[...]],
        rtable,
        pick_remote,
        gathered,
        faces,
        face_kind,
        orientation,
        worient,
        x3o,
        other,
        flux_sum,
        flux_neighbor,
        x3l,
        wlift,
        volume,
        emit,
    )


def call(kernel, args, outs, scratch, flops, spaces=None, out_spaces=None, far=()):
    whole = pl.BlockSpec(memory_space=pltpu.VMEM)
    spaces = spaces or {}
    out_spaces = out_spaces or {}
    args = [
        pltpu.with_memory_space_constraint(x, pltpu.HBM if i in far else pltpu.VMEM)
        for i, x in enumerate(args)
    ]
    return pl.pallas_call(
        kernel,
        out_shape=outs,
        in_specs=[spaces.get(i, whole) for i in range(len(args))],
        out_specs=tuple(out_spaces.get(i, whole) for i in range(len(outs))),
        scratch_shapes=scratch,
        compiler_params=pltpu.CompilerParams(vmem_limit_bytes=VMEM_LIMIT),
        cost_estimate=pl.CostEstimate(flops=flops, bytes_accessed=4000000, transcendentals=0),
    )(*args)


def keep(*shape, dtype=F32):
    return pltpu.VMEM(shape, dtype)


def deliver(outgoing):
    received = []
    for value, by in zip(outgoing, (2, 1, -1, -2)):
        length = lax.axis_size("dom")
        pairs = [(i, (i + by) % length) for i in range(length)]
        received.append(lax.ppermute(value, "dom", pairs))
    return received


def shards(
    fwd_dofs,
    adj_dofs,
    star,
    flux_local,
    flux_neighbor,
    timescale,
    cluster,
    face_kind,
    neighbor_index,
    neighbor_face,
    orientation,
    send_element,
    send_face,
    stiffness,
    face_proj,
    face_lift,
    face_orient,
):
    count = lax.axis_size("dom")
    halves = jnp.minimum(timescale[:HALF], timescale[HALF:])
    steps = lax.all_to_all(jnp.broadcast_to(halves[None], (count, HALF)), "dom", 0, 0)
    cluster = cluster.reshape(1, ELEMS)

    fwd_dofs = jnp.transpose(fwd_dofs, (1, 0, 2))
    adj_dofs = jnp.transpose(adj_dofs, (1, 0, 2))
    star = jnp.transpose(star, (1, 2, 0, 3))
    flux_local = jnp.transpose(flux_local, (1, 2, 0, 3))
    flux_neighbor = jnp.transpose(flux_neighbor, (1, 2, 0, 3))
    face_proj = jnp.transpose(face_proj, (1, 0, 2))
    face_lift = jnp.transpose(face_lift, (2, 0, 1))

    bf16 = {"dtype": BF16}
    whole = pl.BlockSpec(memory_space=pltpu.VMEM)
    away = pl.BlockSpec(memory_space=pl.ANY)
    message = keep(TABLE, HALF)
    face_data = keep(2, QUANT, 4 * FROWS, ELEMS)
    table_data = keep(4 * TABLE, 4 * ELEMS, **bf16)
    stacked = keep(2, QUANT, 3 * PACK, ELEMS, **bf16)
    fields = keep(2, QUANT, ROWS, ELEMS)
    apart = (ORDER - 1, 2, QUANT, ROWS, ELEMS)
    spread = keep(QUANT, 3 * ROWS, ELEMS)
    remote_scratch = (
        keep(4 * TABLE, ELEMS, **bf16),
        keep(2, 4, QUANT, 3 * FROWS, ELEMS, **bf16),
        face_data,
        keep(QUANT, 12 * FROWS, ELEMS, **bf16),
    )

    (
        derived,
        pick_local,
        pick_remote,
        pick_send,
        pick_fine,
        fine_star,
        wstiff,
        wstiff_t,
        wproj,
        wlift,
        worient,
        star,
        flux_local,
        flux_neighbor,
        face_kind,
        orientation,
        cluster,
    ) = call(
        first_kernel,
        (
            fwd_dofs,
            adj_dofs,
            star,
            stiffness,
            face_proj,
            send_element,
            send_face,
            face_kind,
            neighbor_index,
            neighbor_face,
            cluster,
            orientation,
            face_lift,
            face_orient,
            flux_local,
            flux_neighbor,
        ),
        (
            pltpu.HBM(apart, F32),
            pltpu.HBM((4 * ELEMS, 4 * ELEMS), BF16),
            keep(ELEMS, 4 * ELEMS, **bf16),
            keep(4 * ELEMS, ELEMS, **bf16),
            keep(HALF, ELEMS, **bf16),
            keep(QUANT, QUANT, 3, HALF),
            keep(3 * ROWS, 3 * PACK, **bf16),
            keep(3 * ROWS, 3 * PACK, **bf16),
            keep(4 * FROWS, 3 * PACK, **bf16),
            keep(ROWS, 12 * FROWS, **bf16),
            keep(3 * FROWS, 3 * FROWS, **bf16),
            keep(*star.shape),
            keep(*flux_local.shape),
            keep(*flux_neighbor.shape),
            keep(4, ELEMS, dtype=jnp.int32),
            keep(4, ELEMS, dtype=jnp.int32),
            keep(1, ELEMS, dtype=jnp.int32),
        ),
        (
            keep(128, 256),
            keep(QUANT, 3 * PACK, ELEMS, **bf16),
            spread,
            keep(8, ELEMS, dtype=jnp.int32),
            keep(ORDER, 2, QUANT, ROWS, ELEMS),
            pltpu.SemaphoreType.DMA((ORDER + 2,)),
        ),
        14000000000,
        far=range(16),
        spaces={2: away, 14: away, 15: away},
        out_spaces={0: away},
    )

    def local(x3, faces, table):
        return call(
            local_kernel,
            (x3, star, faces, table, flux_local, pick_local, wstiff_t),
            (keep(2, QUANT, ROWS, ELEMS), face_data, keep(2, 4, TABLE, ELEMS)),
            (spread,),
            4000000000,
        )

    *outgoing, integral, later, faces, table, x3 = call(
        integral_kernel,
        (steps, fwd_dofs, adj_dofs, derived, pick_send, wproj),
        (message,) * 4 + (fields, fields, face_data, table_data, stacked),
        (keep(*apart), pltpu.SemaphoreType.DMA((ORDER - 1,))),
        2000000000,
        spaces={3: away},
        far=(1, 2, 3),
    )
    received = deliver(outgoing)
    volume, flux_sum, gathered = local(x3, faces, table)

    *outgoing, base, faces, table, x3, sens = call(
        middle_kernel,
        (
            steps,
            fwd_dofs,
            adj_dofs,
            integral,
            later,
            *received,
            pick_remote,
            pick_send,
            pick_fine,
            fine_star,
            gathered,
            faces,
            face_kind,
            orientation,
            worient,
            flux_sum,
            flux_neighbor,
            wlift,
            volume,
            cluster,
            wstiff,
            wproj,
        ),
        (message,) * 4
        + (keep(2, QUANT, ROWS, ELEMS), face_data, table_data, stacked, keep(1, ELEMS)),
        remote_scratch
        + (
            keep(QUANT, PACK, 4 * ELEMS, **bf16),
            keep(QUANT, 3 * PACK, HALF, **bf16),
            keep(QUANT, 3 * ROWS, HALF),
            keep(QUANT, ROWS, HALF),
        ),
        8000000000,
    )
    received = deliver(outgoing)
    volume, flux_sum, gathered = local(x3, faces, table)

    fwd_final, adj_final = call(
        last_kernel,
        (
            *received,
            pick_remote,
            gathered,
            faces,
            face_kind,
            orientation,
            worient,
            flux_sum,
            flux_neighbor,
            wlift,
            volume,
            base,
            cluster,
        ),
        (
            jax.ShapeDtypeStruct(fwd_dofs.shape, F32),
            jax.ShapeDtypeStruct(adj_dofs.shape, F32),
        ),
        remote_scratch,
        4000000000,
    )
    return (
        jnp.transpose(fwd_final, (1, 0, 2)),
        jnp.transpose(adj_final, (1, 0, 2)),
        sens.reshape(ELEMS),
    )


def solution(mesh):
    return jax.shard_map(
        shards,
        mesh=mesh,
        in_specs=(
            P(None, None, "dom"),
            P(None, None, "dom"),
            P(None, None, None, "dom"),
            P(None, None, None, "dom"),
            P(None, None, None, "dom"),
            P("dom"),
            P("dom"),
            P(None, "dom"),
            P(None, "dom"),
            P(None, "dom"),
            P(None, "dom"),
            P(None, "dom"),
            P(None, "dom"),
            P(),
            P(),
            P(),
            P(),
        ),
        out_specs=(P(None, None, "dom"), P(None, None, "dom"), P("dom")),
        check_vma=False,
    )
```

profile of v0, /device:TPU:1, one launch (start us, length us, event | category | flops | bytes accessed | tf_op | source)
XLA Modules:
  0.0 73.3 jit_solution(12221704887621958628)
XLA Ops:
  0.6 0.8 %slice_minimum_fusion = f32[128]{0:T(128)S(1)} fusion(f32[256]{0:T(256)} %param.22), kind=kLoop, calls=%fused_computation | loop fusion | flops 128 | bytes 1536 | tf_op jit(solution)/shard_map/min | solution.py:708
  1.4 0.7 broadcast_in_dim.2
  2.1 15.7 %all-to-all-start = ((f32[256,1,128]{2,1,0:T(1,128)}), f32[256,1,128]{2,1,0:T(1,128)S(1)}, u32[]{:S(2)}, u32[]{:S(2)}) async-start(f32[256,1,128]{2,1,0:T(1,128)} %broadcast_in_dim.2), calls=%async_computation | async-start | bytes 262144 | tf_op jit(solution)/shard_map/all_to_all | solution.py:709
  17.8 14.5 %shard_map.184 = (f32[4,2,9,40,256]{4,3,2,1,0:T(8,128)}, bf16[1024,1024]{1,0:T(8,128)(2,1)}, bf16[256,1024]{1,0:T(8,128)(2,1)S(1)}, bf16[1024,256]{1,0:T(8,128)(...) custom-call(f32[9,35,256]{2,1,0:T(8,128)} %bitcast.15, ...), custom_call_target="tpu_custom_call" | custom-call | flops 14000000000 | bytes 4000000 | tf_op jit(solution)/shard_map/pallas_call | solution.py:664
  32.3 0.0 all-to-all-done
  32.3 0.0 copy-start.2
  32.3 4.3 %shard_map.185 = (f32[144,128]{1,0:T(8,128)S(1)}, f32[144,128]{1,0:T(8,128)S(1)}, f32[144,128]{1,0:T(8,128)S(1)}, f32[144,128]{1,0:T(8,128)S(1)}, f32[2,9,40,256...) custom-call(f32[256,128]{1,0:T(8,128)S(1)} %bitcast.13, ...), custom_call_target="tpu_custom_call" | custom-call | flops 2000000000 | bytes 4000000 | tf_op jit(solution)/shard_map/pallas_call | solution.py:664
  36.6 1.5 %collective-permute-start = (f32[144,128]{1,0:T(8,128)S(1)}, f32[144,128]{1,0:T(8,128)S(1)}, u32[]{:S(2)}, u32[]{:S(2)}) collective-permute-start(f32[144,128]{1,0:T(8,128)S(1)} %get-tuple-element.51), channel_id=1, source_target_pairs={{0,2},{1,3},{2,4},{3,5},{4,6},{5,7},{6,8},{7,9},{8,10},{9,11},{10,... | collective-permute-start | bytes 221192 | tf_op jit(solution)/shard_map/ppermute | solution.py:684
  38.1 1.7 %collective-permute-start.1 = (f32[144,128]{1,0:T(8,128)S(1)}, f32[144,128]{1,0:T(8,128)S(1)}, u32[]{:S(2)}, u32[]{:S(2)}) collective-permute-start(f32[144,128]{1,0:T(8,128)S(1)} %get-tuple-element.52), channel_id=1, source_target_pairs={{0,1},{1,2},{2,3},{3,4},{4,5},{5,6},{6,7},{7,8},{8,9},{9,10},{10,1... | collective-permute-start | bytes 221192 | tf_op jit(solution)/shard_map/ppermute | solution.py:684
  39.8 0.0 collective-permute-start.2
  39.8 6.3 %collective-permute-start.3 = (f32[144,128]{1,0:T(8,128)S(1)}, f32[144,128]{1,0:T(8,128)S(1)}, u32[]{:S(2)}, u32[]{:S(2)}) collective-permute-start(f32[144,128]{1,0:T(8,128)S(1)} %get-tuple-element.54), channel_id=1, source_target_pairs={{0,254},{1,255},{2,0},{3,1},{4,2},{5,3},{6,4},{7,5},{8,6},{9,7},{1... | collective-permute-start | bytes 221192 | tf_op jit(solution)/shard_map/ppermute | solution.py:684
  46.1 0.0 copy-done.2
  46.1 0.0 copy-start
  46.1 0.0 copy-start.1
  46.1 3.8 %shard_map.186 = (f32[2,9,40,256]{3,2,1,0:T(8,128)S(1)}, f32[2,9,64,256]{3,2,1,0:T(8,128)S(1)}, f32[2,4,144,256]{3,2,1,0:T(8,128)S(1)}) custom-call(bf16[2,9,144,256]{3,2,1,0:T(8,128)(2,1)S(1)} %get-tuple-element.58.x3, f32[9,9,3,256]{3,2,1,0:T(4,128)S(1)} %get-tuple-element.59.star, f32[2,9,64,256]{3,2,1,0:T(8,128)S(1)} %get-tuple-element.60.faces, ...), custom_call_target="tpu_custom_call" | custom-call | flops 4000000000 | bytes 4000000 | tf_op jit(solution)/shard_map/pallas_call | solution.py:664
  49.9 0.0 collective-permute-done.in0
  49.9 0.0 collective-permute-done.1.in1
  49.9 0.0 collective-permute-done.2.in2
  49.9 0.0 collective-permute-done.3.in3
  49.9 0.0 copy-done
  49.9 0.0 copy-done.1
  50.0 6.4 %shard_map.187 = (f32[144,128]{1,0:T(8,128)S(1)}, f32[144,128]{1,0:T(8,128)S(1)}, f32[144,128]{1,0:T(8,128)S(1)}, f32[144,128]{1,0:T(8,128)S(1)}, f32[2,9,40,256...) custom-call(f32[256,128]{1,0:T(8,128)S(1)} %bitcast.14, ...), custom_call_target="tpu_custom_call" | custom-call | flops 8000000000 | bytes 4000000 | tf_op jit(solution)/shard_map/pallas_call | solution.py:664
  56.4 0.1 collective-permute-start.4
  56.5 1.7 %collective-permute-start.5 = (f32[144,128]{1,0:T(8,128)S(1)}, f32[144,128]{1,0:T(8,128)S(1)}, u32[]{:S(2)}, u32[]{:S(2)}) collective-permute-start(f32[144,128]{1,0:T(8,128)S(1)} %get-tuple-element.76), channel_id=1, source_target_pairs={{0,1},{1,2},{2,3},{3,4},{4,5},{5,6},{6,7},{7,8},{8,9},{9,10},{10,1... | collective-permute-start | bytes 221192 | tf_op jit(solution)/shard_map/ppermute | solution.py:684
  58.2 0.4 collective-permute-start.6
  58.6 7.0 %collective-permute-start.7 = (f32[144,128]{1,0:T(8,128)S(1)}, f32[144,128]{1,0:T(8,128)S(1)}, u32[]{:S(2)}, u32[]{:S(2)}) collective-permute-start(f32[144,128]{1,0:T(8,128)S(1)} %get-tuple-element.78), channel_id=1, source_target_pairs={{0,254},{1,255},{2,0},{3,1},{4,2},{5,3},{6,4},{7,5},{8,6},{9,7},{1... | collective-permute-start | bytes 221192 | tf_op jit(solution)/shard_map/ppermute | solution.py:684
  65.6 3.8 %shard_map.188 = (f32[2,9,40,256]{3,2,1,0:T(8,128)S(1)}, f32[2,9,64,256]{3,2,1,0:T(8,128)S(1)}, f32[2,4,144,256]{3,2,1,0:T(8,128)S(1)}) custom-call(bf16[2,9,144,256]{3,2,1,0:T(8,128)(2,1)S(1)} %get-tuple-element.79.x3, f32[9,9,3,256]{3,2,1,0:T(4,128)S(1)} %get-tuple-element.59.star, f32[2,9,64,256]{3,2,1,0:T(8,128)S(1)} %get-tuple-element.80.faces, ...), custom_call_target="tpu_custom_call" | custom-call | flops 4000000000 | bytes 4000000 | tf_op jit(solution)/shard_map/pallas_call | solution.py:664
  69.4 0.6 copy.20
  69.9 0.0 collective-permute-done.4.in0
  69.9 0.0 collective-permute-done.5.in1
  70.0 0.0 collective-permute-done.6.in2
  70.0 0.0 collective-permute-done.7.in3
  70.0 3.4 %shard_map.189 = (f32[9,35,256]{2,1,0:T(8,128)}, f32[9,35,256]{2,1,0:T(8,128)}) custom-call(f32[144,128]{1,0:T(8,128)S(1)} %collective-permute-done.4.in0, f32[144,128]{1,0:T(8,128)S(1)} %collective-permute-done.5.in1, f32[144,128]{1,0:T(8,128)S(1)} %collective-permute-done.6.in2, f32[144,128]{1,0:T(8,128)S(1)} %collective-permute-done.7.in3, ...), custom_call_target="tpu_custom_call" | custom-call | flops 4000000000 | bytes 4000000 | tf_op jit(solution)/shard_map/pallas_call | solution.py:664
Async XLA Ops:
  2.1 30.1 %all-to-all-start = ((f32[256,1,128]{2,1,0:T(1,128)}), f32[256,1,128]{2,1,0:T(1,128)S(1)}, u32[]{:S(2)}, u32[]{:S(2)}) async-start(f32[256,1,128]{2,1,0:T(1,128)} %broadcast_in_dim.2), calls=%async_computation | async-start | bytes 262144 | tf_op jit(solution)/shard_map/all_to_all | solution.py:709
  32.3 13.8 %copy-start.2 = (bf16[1024,1024]{1,0:T(8,128)(2,1)S(1)}, bf16[1024,1024]{1,0:T(8,128)(2,1)}, u32[]{:S(2)}) copy-start(bf16[1024,1024]{1,0:T(8,128)(2,1)} %get-tuple-element.63.pick_local) | copy-start | bytes 6291460
  36.6 13.3 %collective-permute-start = (f32[144,128]{1,0:T(8,128)S(1)}, f32[144,128]{1,0:T(8,128)S(1)}, u32[]{:S(2)}, u32[]{:S(2)}) collective-permute-start(f32[144,128]{1,0:T(8,128)S(1)} %get-tuple-element.51), channel_id=1, source_target_pairs={{0,2},{1,3},{2,4},{3,5},{4,6},{5,7},{6,8},{7,9},{8,10},{9,11},{10,... | collective-permute-start | bytes 221192 | tf_op jit(solution)/shard_map/ppermute | solution.py:684
  38.1 11.8 %collective-permute-start.1 = (f32[144,128]{1,0:T(8,128)S(1)}, f32[144,128]{1,0:T(8,128)S(1)}, u32[]{:S(2)}, u32[]{:S(2)}) collective-permute-start(f32[144,128]{1,0:T(8,128)S(1)} %get-tuple-element.52), channel_id=1, source_target_pairs={{0,1},{1,2},{2,3},{3,4},{4,5},{5,6},{6,7},{7,8},{8,9},{9,10},{10,1... | collective-permute-start | bytes 221192 | tf_op jit(solution)/shard_map/ppermute | solution.py:684
  39.8 10.1 %collective-permute-start.2 = (f32[144,128]{1,0:T(8,128)S(1)}, f32[144,128]{1,0:T(8,128)S(1)}, u32[]{:S(2)}, u32[]{:S(2)}) collective-permute-start(f32[144,128]{1,0:T(8,128)S(1)} %get-tuple-element.53), channel_id=1, source_target_pairs={{0,255},{1,0},{2,1},{3,2},{4,3},{5,4},{6,5},{7,6},{8,7},{9,8},{10,... | collective-permute-start | bytes 221192 | tf_op jit(solution)/shard_map/ppermute | solution.py:684
  39.8 10.1 %collective-permute-start.3 = (f32[144,128]{1,0:T(8,128)S(1)}, f32[144,128]{1,0:T(8,128)S(1)}, u32[]{:S(2)}, u32[]{:S(2)}) collective-permute-start(f32[144,128]{1,0:T(8,128)S(1)} %get-tuple-element.54), channel_id=1, source_target_pairs={{0,254},{1,255},{2,0},{3,1},{4,2},{5,3},{6,4},{7,5},{8,6},{9,7},{1... | collective-permute-start | bytes 221192 | tf_op jit(solution)/shard_map/ppermute | solution.py:684
  46.1 3.8 %copy-start = (f32[35,9,256]{2,0,1:T(8,128)S(1)}, f32[35,9,256]{2,0,1:T(8,128)}, u32[]{:S(2)}) copy-start(f32[35,9,256]{2,0,1:T(8,128)} %param.17) | copy-start | bytes 967684
  46.1 3.8 %copy-start.1 = (f32[35,9,256]{2,0,1:T(8,128)S(1)}, f32[35,9,256]{2,0,1:T(8,128)}, u32[]{:S(2)}) copy-start(f32[35,9,256]{2,0,1:T(8,128)} %param.18) | copy-start | bytes 967684
  56.4 13.6 %collective-permute-start.4 = (f32[144,128]{1,0:T(8,128)S(1)}, f32[144,128]{1,0:T(8,128)S(1)}, u32[]{:S(2)}, u32[]{:S(2)}) collective-permute-start(f32[144,128]{1,0:T(8,128)S(1)} %get-tuple-element.75), channel_id=1, source_target_pairs={{0,2},{1,3},{2,4},{3,5},{4,6},{5,7},{6,8},{7,9},{8,10},{9,11},{10,... | collective-permute-start | bytes 221192 | tf_op jit(solution)/shard_map/ppermute | solution.py:684
  56.5 13.5 %collective-permute-start.5 = (f32[144,128]{1,0:T(8,128)S(1)}, f32[144,128]{1,0:T(8,128)S(1)}, u32[]{:S(2)}, u32[]{:S(2)}) collective-permute-start(f32[144,128]{1,0:T(8,128)S(1)} %get-tuple-element.76), channel_id=1, source_target_pairs={{0,1},{1,2},{2,3},{3,4},{4,5},{5,6},{6,7},{7,8},{8,9},{9,10},{10,1... | collective-permute-start | bytes 221192 | tf_op jit(solution)/shard_map/ppermute | solution.py:684
  58.2 11.8 %collective-permute-start.6 = (f32[144,128]{1,0:T(8,128)S(1)}, f32[144,128]{1,0:T(8,128)S(1)}, u32[]{:S(2)}, u32[]{:S(2)}) collective-permute-start(f32[144,128]{1,0:T(8,128)S(1)} %get-tuple-element.77), channel_id=1, source_target_pairs={{0,255},{1,0},{2,1},{3,2},{4,3},{5,4},{6,5},{7,6},{8,7},{9,8},{10,... | collective-permute-start | bytes 221192 | tf_op jit(solution)/shard_map/ppermute | solution.py:684
  58.6 11.4 %collective-permute-start.7 = (f32[144,128]{1,0:T(8,128)S(1)}, f32[144,128]{1,0:T(8,128)S(1)}, u32[]{:S(2)}, u32[]{:S(2)}) collective-permute-start(f32[144,128]{1,0:T(8,128)S(1)} %get-tuple-element.78), channel_id=1, source_target_pairs={{0,254},{1,255},{2,0},{3,1},{4,2},{5,3},{6,4},{7,5},{8,6},{9,7},{1... | collective-permute-start | bytes 221192 | tf_op jit(solution)/shard_map/ppermute | solution.py:684
where the time goes:
time: 73.6 us; the launch traced here: 73.3 us
  Pallas kernels  36.1 us (49%)
  starting transfers between devices  34.3 us (47%)
  local copies, waits for them, and re-layouts  1.3 us (2%)
  between operations  0.77 us (1%)
  other arithmetic  0.76 us (1%)
    pallas_call x6, Pallas kernels, call(): pl.pallas_call(kernel, out_shape=outs, in_specs=[spaces.get(i, whole) for...  36.1 us
    ppermute x8, starting transfers between devices, deliver(): received.append(lax.ppermute(value, 'dom', pairs))  18.7 us
    all_to_all x1, starting transfers between devices, shards(): lax.all_to_all(jnp.broadcast_to(halves[None], (count, HALF)), 'dom', 0, 0)  15.7 us
  transfers between devices with their start and end apart: 9, of which 0 were waited for; matrix products, arithmetic and copies ran while one was open for 1% of the time, Pallas kernels for 30%

commit v1 on v0

--- a/solution.py
+++ b/solution.py
@@ -96,6 +96,14 @@
     x3[q, 0:PACK, :] = hi
     x3[q, PACK : 2 * PACK, :] = lo
     x3[q, 2 * PACK : 3 * PACK, :] = hi
+
+
+def stack_pair(x3, q, x):
+    hi, lo = split(jnp.concatenate([x, jnp.zeros((PACK - ROWS, HALF), F32)], 0))
+    lanes = slice(q % 2 * HALF, q % 2 * HALF + HALF)
+    x3[q // 2, 0:PACK, lanes] = hi
+    x3[q // 2, PACK : 2 * PACK, lanes] = lo
+    x3[q // 2, 2 * PACK : 3 * PACK, lanes] = hi
 
 
 def star_apply(spread, star, adjoint, half, emit):
@@ -188,7 +196,8 @@
     pick_local,
     pick_remote,
     pick_send,
-    pick_fine,
+    take_fine,
+    give_fine,
     fine_star,
     wstiff,
     wstiff_t,
@@ -206,15 +215,20 @@
     spread,
     codes,
     series,
+    raw,
+    local_picks,
     sems,
 ):
     copies = [
-        pltpu.make_async_copy(source, kept, sems.at[ORDER - 1 + i])
+        pltpu.make_async_copy(source, kept, sems.at[2, i])
         for i, (source, kept) in enumerate(
             ((star, star_kept), (flux_local, local_kept), (flux_neighbor, neighbor_kept))
         )
     ]
-    for copy in copies:
+    loads = [
+        pltpu.make_async_copy(field, raw.at[n], sems.at[3, n]) for n, field in enumerate((fwd, adj))
+    ]
+    for copy in loads + copies:
         copy.start()
     star = star_kept
     kind_kept[...] = face_kind[...]
@@ -225,11 +239,6 @@
     fill_proj(wproj, stage, face_proj)
     fill_lift(wlift, stage, face_lift)
     fill_orient(worient, stage, face_orient)
-
-    for n, field in enumerate((fwd, adj)):
-        for q in range(QUANT):
-            series[0, n, q, 0:BASIS, :] = field[q]
-            series[0, n, q, BASIS:ROWS, :] = jnp.zeros((ROWS - BASIS, ELEMS), F32)
 
     send_code = send_face[...] * ELEMS + send_element[...]
     for g in range(4):
@@ -245,8 +254,10 @@
         remote = jnp.where(kind == 1, index, -1)
         for block in range(4):
             rows = slice(block * ELEMS, block * ELEMS + ELEMS)
-            pick_local[rows, lanes] = one_hot(local, block * ELEMS, ELEMS)
+            local_picks[rows, lanes] = one_hot(local, block * ELEMS, ELEMS)
         pick_remote[:, lanes] = one_hot(remote, 0, ELEMS)
+    table_out = pltpu.make_async_copy(local_picks, pick_local, sems.at[3, 2])
+    table_out.start()
 
     fine = cluster[...] == 0
     upper = lax.broadcasted_iota(jnp.int32, (ELEMS, ELEMS), 0) < lax.broadcasted_iota(
@@ -258,8 +269,12 @@
     slot = lax.broadcasted_iota(jnp.int32, (HALF, ELEMS), 0)
     slot = jnp.where(slot < SLOTS, slot, slot - SLOTS)
     chosen = jnp.where(slot == place_of, 1.0, 0.0)
-    pick_fine[...] = chosen.astype(BF16)
     pick_t = chosen.T.astype(BF16)
+    below = lax.broadcasted_iota(jnp.int32, (HALF, ELEMS), 0) < SLOTS
+    for n in range(2):
+        own = jnp.where(below, chosen, 0.0) if n == 0 else jnp.where(below, 0.0, chosen)
+        give_fine[n] = own.astype(BF16)
+        take_fine[n] = own.T.astype(BF16)
     low1 = lax.broadcasted_iota(jnp.int32, (1, HALF), 1) < SLOTS
     copies[0].wait()
     for d in range(3):
@@ -273,6 +288,12 @@
                     low1, plain[q][p : p + 1], plain[p][q : q + 1]
                 )
 
+    for n in range(2):
+        loads[n].wait()
+        for q in range(QUANT):
+            series[0, n, q, 0:BASIS, :] = raw[n, q]
+            series[0, n, q, BASIS:ROWS, :] = jnp.zeros((ROWS - BASIS, ELEMS), F32)
+
     def step(degree, _):
         for n in range(2):
             for q in range(QUANT):
@@ -285,18 +306,25 @@
                     series[degree + 1, n, q, :, lanes] = value
 
                 star_apply(spread, star, n == 1, half, emit)
-        pltpu.make_async_copy(series.at[degree + 1], derived.at[degree], sems.at[degree]).start()
+        for n in range(2):
+            pltpu.make_async_copy(
+                series.at[degree + 1, n], derived.at[n, degree], sems.at[n, degree]
+            ).start()
         return 0
 
     lax.fori_loop(0, ORDER - 1, step, 0)
     copies[1].wait()
     copies[2].wait()
-    for degree in range(ORDER - 1):
-        pltpu.make_async_copy(series.at[degree + 1], derived.at[degree], sems.at[degree]).wait()
-
-
-def weights_of(steps):
-    dt = 0.5 * jnp.min(steps[...])
+    table_out.wait()
+    for n in range(2):
+        for degree in range(ORDER - 1):
+            pltpu.make_async_copy(
+                series.at[degree + 1, n], derived.at[n, degree], sems.at[n, degree]
+            ).wait()
+
+
+def weights_of(smallest):
+    dt = 0.5 * smallest
     early = []
     late = []
     power = dt
@@ -320,38 +348,44 @@
     out2,
     out3,
     integral,
-    later,
     faces,
     table,
     x3,
     series,
+    start,
+    least,
     sems,
 ):
     outs = (out0, out1, out2, out3)
-    copies = [
-        pltpu.make_async_copy(derived.at[degree], series.at[degree], sems.at[degree])
-        for degree in range(ORDER - 1)
-    ]
-    for copy in copies:
-        copy.start()
-    early, late = weights_of(steps)
+    third = QUANT // 3
+    starts = []
+    copies = []
     for n, field in enumerate((fwd, adj)):
+        starts.append(pltpu.make_async_copy(field, start.at[n], sems.at[n, 3]))
+        starts[n].start()
+        copies.append([])
+        for part in range(3):
+            some = slice(part * third, part * third + third)
+            copies[n].append(
+                pltpu.make_async_copy(
+                    derived.at[n, :, some], series.at[n, :, some], sems.at[n, part]
+                )
+            )
+            copies[n][part].start()
+    smallest = jnp.min(steps[...])
+    least[...] = jnp.full(least.shape, smallest, F32)
+    early, _ = weights_of(smallest)
+    for n in range(2):
+        starts[n].wait()
         for q in range(QUANT):
-            for sums, weight in ((integral, early[0]), (later, late[0])):
-                sums[n, q, 0:BASIS, :] = weight * field[q]
-                sums[n, q, BASIS:ROWS, :] = jnp.zeros((ROWS - BASIS, ELEMS), F32)
-    for copy in copies:
-        copy.wait()
-    for n in range(2):
-        for q in range(QUANT):
+            if q % third == 0:
+                copies[n][q // third].wait()
+            integral[n, q, 0:BASIS, :] = early[0] * start[n, q]
+            integral[n, q, BASIS:ROWS, :] = jnp.zeros((ROWS - BASIS, ELEMS), F32)
             total = integral[n, q]
-            after = later[n, q]
             for degree in range(1, ORDER):
-                value = series[degree - 1, n, q]
-                total = total + early[degree] * value
-                after = after + late[degree] * value
+                total = total + early[degree] * series[n, degree - 1, q]
             integral[n, q] = total
-            later[n, q] = after
             stack_split(x3.at[n], q, total)
         project(x3.at[n], wproj, table, n, faces)
 
@@ -474,9 +508,8 @@
 
 
 def middle_kernel(
-    steps,
-    fwd,
-    adj,
+    least,
+    start,
     integral,
     later,
     in0,
@@ -485,7 +518,8 @@
     in3,
     pick_remote,
     pick_send,
-    pick_fine,
+    take_fine,
+    give_fine,
     fine_star,
     gathered,
     faces,
@@ -518,19 +552,19 @@
     fields_c,
 ):
     outs = (out0, out1, out2, out3)
-    early, _ = weights_of(steps)
+    early, _ = weights_of(jnp.min(least[...]))
+    x3c[QUANT // 2, :, HALF:] = jnp.zeros((3 * PACK, HALF), BF16)
     fine = cluster[...] == 0
     active = cluster[...] <= 1
 
     def emit_first(n, q, value):
-        start = jnp.concatenate([(fwd, adj)[n][q], jnp.zeros((ROWS - BASIS, ELEMS), F32)], 0)
-        moved = start + value
-        base[n, q] = jnp.where(active, moved, start)
-        hi, lo = split(moved)
-        wide[q, 0:ROWS, 2 * n * ELEMS : (2 * n + 1) * ELEMS] = hi
-        wide[q, 0:ROWS, (2 * n + 1) * ELEMS : (2 * n + 2) * ELEMS] = lo
-
-    wide[...] = jnp.zeros(wide.shape, BF16)
+        before = jnp.concatenate([start[n, q], jnp.zeros((ROWS - BASIS, ELEMS), F32)], 0)
+        moved = before + value
+        base[n, q] = jnp.where(active, moved, before)
+        hi, lo = split(jnp.concatenate([moved, jnp.zeros((PACK - ROWS, ELEMS), F32)], 0))
+        wide[q, :, 2 * n * ELEMS : (2 * n + 1) * ELEMS] = hi
+        wide[q, :, (2 * n + 1) * ELEMS : (2 * n + 2) * ELEMS] = lo
+
     remote_part(
         [in0[...], in1[...], in2[...], in3[...]],
         rtable,
@@ -550,36 +584,36 @@
         emit_first,
     )
 
-    slot = lax.broadcasted_iota(jnp.int32, (HALF, ELEMS), 0)
-    chosen = pick_fine[...].astype(F32)
-    mine = [jnp.where(slot < SLOTS, chosen, 0.0), jnp.where(slot < SLOTS, 0.0, chosen)]
-    pick_t = [m.T.astype(BF16) for m in mine]
-    mine = [m.astype(BF16) for m in mine]
     for q in range(QUANT):
         value = jnp.zeros((ROWS, HALF), F32)
         for n in range(2):
             for part in range(2):
                 lanes = slice((2 * n + part) * ELEMS, (2 * n + part + 1) * ELEMS)
-                value = value + dot(wide[q, :, lanes], pick_t[n])[0:ROWS]
+                value = value + dot(wide[q, :, lanes], take_fine[n])[0:ROWS]
         fields_c[q] = early[0] * value
-        stack_split(x3c, q, value)
+        stack_pair(x3c, q, value)
     for degree in range(1, ORDER):
+        for pair in range((QUANT + 1) // 2):
+            spread_c[pair] = dot(wstiff[...], x3c[pair])
+        acc = [None] * QUANT
+        for p in range(QUANT):
+            side = slice(p % 2 * HALF, p % 2 * HALF + HALF)
+            for d in range(3):
+                value = spread_c[p // 2, d * ROWS : d * ROWS + ROWS, side]
+                for q in range(QUANT):
+                    term = value * fine_star[q, p, d : d + 1, :]
+                    acc[q] = term if acc[q] is None else acc[q] + term
         for q in range(QUANT):
-            spread_c[q] = dot(wstiff[...], x3c[q])
-
-        def emit(q, lanes, value):
-            fields_c[q] = fields_c[q] + early[degree] * value
+            fields_c[q] = fields_c[q] + early[degree] * acc[q]
             if degree < ORDER - 1:
-                stack_split(x3c, q, value)
-
-        star_apply(spread_c, fine_star, False, 0, emit)
+                stack_pair(x3c, q, acc[q])
 
     products = jnp.zeros((ROWS, ELEMS), F32)
     for q in range(QUANT):
         hi, lo = split(jnp.concatenate([fields_c[q], jnp.zeros((PACK - ROWS, HALF), F32)], 0))
         both = []
         for n in range(2):
-            renewed = (dot(hi, mine[n]) + dot(lo, mine[n]))[0:ROWS]
+            renewed = (dot(hi, give_fine[n]) + dot(lo, give_fine[n]))[0:ROWS]
             value = jnp.where(fine, renewed, later[n, q])
             stack_split(x3.at[n], q, value)
             both.append(value)
@@ -600,6 +634,37 @@
     local_part(
         x3, wstiff_t, spread, star, faces, table, flux_local, pick_local, volume, flux_sum, gathered
     )
+
+
+def first_local_kernel(
+    x3,
+    star,
+    faces,
+    table,
+    flux_local,
+    pick_local,
+    wstiff_t,
+    least,
+    start,
+    series,
+    volume,
+    flux_sum,
+    gathered,
+    later,
+    spread,
+):
+    local_part(
+        x3, wstiff_t, spread, star, faces, table, flux_local, pick_local, volume, flux_sum, gathered
+    )
+    _, late = weights_of(jnp.min(least[...]))
+    for n in range(2):
+        for q in range(QUANT):
+            later[n, q, 0:BASIS, :] = late[0] * start[n, q]
+            later[n, q, BASIS:ROWS, :] = jnp.zeros((ROWS - BASIS, ELEMS), F32)
+            total = later[n, q]
+            for degree in range(1, ORDER):
+                total = total + late[degree] * series[n, degree - 1, q]
+            later[n, q] = total
 
 
 def last_kernel(
@@ -619,19 +684,29 @@
     volume,
     base,
     cluster,
+    sens,
     fwd,
     adj,
+    sens_out,
+    final,
+    sems,
     rtable,
     x3o,
     other,
     x3l,
 ):
     active = cluster[...] <= 1
-    outs = (fwd, adj)
+    copies = [
+        pltpu.make_async_copy(final.at[n], out, sems.at[n]) for n, out in enumerate((fwd, adj))
+    ]
+    copies.append(pltpu.make_async_copy(sens, sens_out, sems.at[2]))
+    copies[2].start()
 
     def emit(n, q, value):
-        final = base[n, q] + jnp.where(active, value, 0.0)
-        outs[n][q] = final[0:BASIS]
+        done = base[n, q] + jnp.where(active, value, 0.0)
+        final[n, q] = done[0:BASIS]
+        if q == QUANT - 1:
+            copies[n].start()
 
     remote_part(
         [in0[...], in1[...], in2[...], in3[...]],
@@ -651,6 +726,8 @@
         volume,
         emit,
     )
+    for copy in copies:
+        copy.wait()
 
 
 def call(kernel, args, outs, scratch, flops, spaces=None, out_spaces=None, far=()):
@@ -705,8 +782,7 @@
     face_orient,
 ):
     count = lax.axis_size("dom")
-    halves = jnp.minimum(timescale[:HALF], timescale[HALF:])
-    steps = lax.all_to_all(jnp.broadcast_to(halves[None], (count, HALF)), "dom", 0, 0)
+    steps = lax.all_to_all(jnp.broadcast_to(timescale, (count, 1, ELEMS)), "dom", 0, 0)
     cluster = cluster.reshape(1, ELEMS)
 
     fwd_dofs = jnp.transpose(fwd_dofs, (1, 0, 2))
@@ -725,7 +801,7 @@
     table_data = keep(4 * TABLE, 4 * ELEMS, **bf16)
     stacked = keep(2, QUANT, 3 * PACK, ELEMS, **bf16)
     fields = keep(2, QUANT, ROWS, ELEMS)
-    apart = (ORDER - 1, 2, QUANT, ROWS, ELEMS)
+    apart = (2, ORDER - 1, QUANT, ROWS, ELEMS)
     spread = keep(QUANT, 3 * ROWS, ELEMS)
     remote_scratch = (
         keep(4 * TABLE, ELEMS, **bf16),
@@ -739,7 +815,8 @@
         pick_local,
         pick_remote,
         pick_send,
-        pick_fine,
+        take_fine,
+        give_fine,
         fine_star,
         wstiff,
         wstiff_t,
@@ -777,7 +854,8 @@
             pltpu.HBM((4 * ELEMS, 4 * ELEMS), BF16),
             keep(ELEMS, 4 * ELEMS, **bf16),
             keep(4 * ELEMS, ELEMS, **bf16),
-            keep(HALF, ELEMS, **bf16),
+            keep(2, ELEMS, HALF, **bf16),
+            keep(2, HALF, ELEMS, **bf16),
             keep(QUANT, QUANT, 3, HALF),
             keep(3 * ROWS, 3 * PACK, **bf16),
             keep(3 * ROWS, 3 * PACK, **bf16),
@@ -797,47 +875,56 @@
             spread,
             keep(8, ELEMS, dtype=jnp.int32),
             keep(ORDER, 2, QUANT, ROWS, ELEMS),
-            pltpu.SemaphoreType.DMA((ORDER + 2,)),
+            keep(2, QUANT, BASIS, ELEMS),
+            keep(4 * ELEMS, 4 * ELEMS, **bf16),
+            pltpu.SemaphoreType.DMA((4, ORDER - 1)),
         ),
         14000000000,
         far=range(16),
-        spaces={2: away, 14: away, 15: away},
-        out_spaces={0: away},
-    )
-
-    def local(x3, faces, table):
-        return call(
-            local_kernel,
-            (x3, star, faces, table, flux_local, pick_local, wstiff_t),
-            (keep(2, QUANT, ROWS, ELEMS), face_data, keep(2, 4, TABLE, ELEMS)),
-            (spread,),
-            4000000000,
-        )
-
-    *outgoing, integral, later, faces, table, x3 = call(
+        spaces={0: away, 1: away, 2: away, 14: away, 15: away},
+        out_spaces={0: away, 1: away},
+    )
+
+    local_out = (fields, face_data, keep(2, 4, TABLE, ELEMS))
+    *outgoing, integral, faces, table, x3, series, start, least = call(
         integral_kernel,
         (steps, fwd_dofs, adj_dofs, derived, pick_send, wproj),
-        (message,) * 4 + (fields, fields, face_data, table_data, stacked),
-        (keep(*apart), pltpu.SemaphoreType.DMA((ORDER - 1,))),
+        (message,) * 4
+        + (
+            fields,
+            face_data,
+            table_data,
+            stacked,
+            keep(*apart),
+            keep(2, QUANT, BASIS, ELEMS),
+            keep(8, HALF),
+        ),
+        (pltpu.SemaphoreType.DMA((2, 4)),),
         2000000000,
-        spaces={3: away},
+        spaces={1: away, 2: away, 3: away},
         far=(1, 2, 3),
     )
     received = deliver(outgoing)
-    volume, flux_sum, gathered = local(x3, faces, table)
+    volume, flux_sum, gathered, later = call(
+        first_local_kernel,
+        (x3, star, faces, table, flux_local, pick_local, wstiff_t, least, start, series),
+        local_out + (fields,),
+        (spread,),
+        4000000000,
+    )
 
     *outgoing, base, faces, table, x3, sens = call(
         middle_kernel,
         (
-            steps,
-            fwd_dofs,
-            adj_dofs,
+            least,
+            start,
             integral,
             later,
             *received,
             pick_remote,
             pick_send,
-            pick_fine,
+            take_fine,
+            give_fine,
             fine_star,
             gathered,
             faces,
@@ -857,16 +944,22 @@
         remote_scratch
         + (
             keep(QUANT, PACK, 4 * ELEMS, **bf16),
-            keep(QUANT, 3 * PACK, HALF, **bf16),
-            keep(QUANT, 3 * ROWS, HALF),
+            keep((QUANT + 1) // 2, 3 * PACK, ELEMS, **bf16),
+            keep((QUANT + 1) // 2, 3 * ROWS, ELEMS),
             keep(QUANT, ROWS, HALF),
         ),
         8000000000,
     )
     received = deliver(outgoing)
-    volume, flux_sum, gathered = local(x3, faces, table)
-
-    fwd_final, adj_final = call(
+    volume, flux_sum, gathered = call(
+        local_kernel,
+        (x3, star, faces, table, flux_local, pick_local, wstiff_t),
+        local_out,
+        (spread,),
+        4000000000,
+    )
+
+    fwd_final, adj_final, sens = call(
         last_kernel,
         (
             *received,
@@ -882,13 +975,16 @@
             volume,
             base,
             cluster,
+            sens,
         ),
         (
-            jax.ShapeDtypeStruct(fwd_dofs.shape, F32),
-            jax.ShapeDtypeStruct(adj_dofs.shape, F32),
+            pltpu.HBM(fwd_dofs.shape, F32),
+            pltpu.HBM(adj_dofs.shape, F32),
+            pltpu.HBM((1, ELEMS), F32),
         ),
-        remote_scratch,
+        (keep(2, QUANT, BASIS, ELEMS), pltpu.SemaphoreType.DMA((3,))) + remote_scratch,
         4000000000,
+        out_spaces={0: away, 1: away, 2: away},
     )
     return (
         jnp.transpose(fwd_final, (1, 0, 2)),

time: 73.6 us -> 71.9 us (0.977)
  Pallas kernels: 36.1 us -> 33.9 us
  waiting for transfers between devices: 0.02 us -> 2.09 us
  starting transfers between devices: 34.3 us -> 33.2 us
  other arithmetic: 0.76 us -> 0 us
    pallas_call x6, Pallas kernels: 36.1 us -> 33.9 us  [call(): pl.pallas_call(kernel, out_shape=outs, in_specs=[spaces.get(i, whole) for...]
    all_to_all x1, waiting for transfers between devices: 0.01 us -> 2.07 us  [shards(): lax.all_to_all(jnp.broadcast_to(timescale, (count, 1, ELEMS)), 'dom', 0, 0)]
    ppermute x8, starting transfers between devices: 18.7 us -> 17.6 us  [deliver(): received.append(lax.ppermute(value, 'dom', pairs))]
    broadcast_in_dim x1, local copies, waits for them, and re-layouts: 0.72 us -> 1.52 us  [shards(): jnp.broadcast_to(timescale, (count, 1, ELEMS))]
    min x1 -> x0, other arithmetic: 0.76 us -> none  [shards(): halves = jnp.minimum(timescale[:HALF], timescale[HALF:])]
  transfers between devices with their start and end apart: 9 -> 9, of which waited for: 0 -> 1; matrix products, arithmetic and copies ran while one was open for 1% -> 0% of each run, Pallas kernels for 30% -> 29%
where the time goes in v1:
time: 71.9 us; the launch traced here: 71.7 us
  Pallas kernels  33.9 us (47%)
  starting transfers between devices  33.2 us (46%)
  waiting for transfers between devices  2.09 us (3%)
  local copies, waits for them, and re-layouts  1.52 us (2%)
  between operations  0.93 us (1%)
    pallas_call x6, Pallas kernels, call(): pl.pallas_call(kernel, out_shape=outs, in_specs=[spaces.get(i, whole) for...  33.9 us
    ppermute x8, starting transfers between devices, deliver(): received.append(lax.ppermute(value, 'dom', pairs))  17.6 us
    all_to_all x1, starting transfers between devices, shards(): lax.all_to_all(jnp.broadcast_to(timescale, (count, 1, ELEMS)), 'dom', 0, 0)  15.7 us
    all_to_all x1, waiting for transfers between devices, shards(): lax.all_to_all(jnp.broadcast_to(timescale, (count, 1, ELEMS)), 'dom', 0, 0)  2.07 us
    broadcast_in_dim x1, local copies, waits for them, and re-layouts, shards(): jnp.broadcast_to(timescale, (count, 1, ELEMS))  1.52 us
  transfers between devices with their start and end apart: 9, of which 1 were waited for; matrix products, arithmetic and copies ran while one was open for 0% of the time, Pallas kernels for 29%

profile of v1, /device:TPU:1, one launch (start us, length us, event | category | flops | bytes accessed | tf_op | source)
XLA Modules:
  0.0 71.7 jit_solution(10413345111783533970)
XLA Ops:
  0.6 1.5 %broadcast_in_dim.3 = f32[256,1,256]{2,1,0:T(1,128)} broadcast(f32[256]{0:T(256)} %param.22), dimensions={2} | broadcast | bytes 263168 | tf_op jit(solution)/shard_map/broadcast_in_dim | solution.py:785
  2.1 15.7 %all-to-all-start = ((f32[256,1,256]{2,1,0:T(1,128)}), f32[256,1,256]{2,1,0:T(1,128)S(1)}, u32[]{:S(2)}, u32[]{:S(2)}) async-start(f32[256,1,256]{2,1,0:T(1,128)} %broadcast_in_dim.3), calls=%async_computation | async-start | bytes 524288 | tf_op jit(solution)/shard_map/all_to_all | solution.py:785
  17.8 13.2 %shard_map.184 = (f32[2,4,9,40,256]{4,3,2,1,0:T(8,128)}, bf16[1024,1024]{1,0:T(8,128)(2,1)}, bf16[256,1024]{1,0:T(8,128)(2,1)S(1)}, bf16[1024,256]{1,0:T(8,128)(...) custom-call(f32[9,35,256]{2,1,0:T(8,128)} %bitcast.11, ...), custom_call_target="tpu_custom_call" | custom-call | flops 14000000000 | bytes 4000000 | tf_op jit(solution)/shard_map/pallas_call | solution.py:741
  31.0 2.1 %all-to-all-done.steps = f32[256,1,256]{2,1,0:T(1,128)S(1)} async-done(((f32[256,1,256]{2,1,0:T(1,128)}), f32[256,1,256]{2,1,0:T(1,128)S(1)}, u32[]{:S(2)}, u32[]{:S(2)}) %all-to-all-start) | async-done | bytes 262176 | tf_op jit(solution)/shard_map/all_to_all | solution.py:785
  33.1 0.0 copy-start
  33.1 2.9 %shard_map.185 = (f32[144,128]{1,0:T(8,128)S(1)}, f32[144,128]{1,0:T(8,128)S(1)}, f32[144,128]{1,0:T(8,128)S(1)}, f32[144,128]{1,0:T(8,128)S(1)}, f32[2,9,40,256...) custom-call(f32[256,1,256]{2,1,0:T(1,128)S(1)} %all-to-all-done.step, ...), custom_call_target="tpu_custom_call" | custom-call | flops 2000000000 | bytes 4000000 | tf_op jit(solution)/shard_map/pallas_call | solution.py:741
  36.0 0.3 collective-permute-start
  36.3 1.2 %collective-permute-start.1 = (f32[144,128]{1,0:T(8,128)S(1)}, f32[144,128]{1,0:T(8,128)S(1)}, u32[]{:S(2)}, u32[]{:S(2)}) collective-permute-start(f32[144,128]{1,0:T(8,128)S(1)} %get-tuple-element.67), channel_id=1, source_target_pairs={{0,1},{1,2},{2,3},{3,4},{4,5},{5,6},{6,7},{7,8},{8,9},{9,10},{10,1... | collective-permute-start | bytes 221192 | tf_op jit(solution)/shard_map/ppermute | solution.py:761
  37.5 0.0 collective-permute-start.2
  37.5 6.8 %collective-permute-start.3 = (f32[144,128]{1,0:T(8,128)S(1)}, f32[144,128]{1,0:T(8,128)S(1)}, u32[]{:S(2)}, u32[]{:S(2)}) collective-permute-start(f32[144,128]{1,0:T(8,128)S(1)} %get-tuple-element.69), channel_id=1, source_target_pairs={{0,254},{1,255},{2,0},{3,1},{4,2},{5,3},{6,4},{7,5},{8,6},{9,7},{1... | collective-permute-start | bytes 221192 | tf_op jit(solution)/shard_map/ppermute | solution.py:761
  44.3 0.0 copy-done
  44.3 4.0 %shard_map.186 = (f32[2,9,40,256]{3,2,1,0:T(8,128)S(1)}, f32[2,9,64,256]{3,2,1,0:T(8,128)S(1)}, f32[2,4,144,256]{3,2,1,0:T(8,128)S(1)}, f32[2,9,40,256]{3,2,1,0:T(8,128)S(1)}) custom-call(bf16[2,9,144,256]{3,2,1,0:T(8,128)(2,1)S(1)} %get-tuple-element.57.x3, f32[9,9,3,256]{3,2,1,0:T(4,128)S(1)} %get-tuple-element.58.star, ...), custom_call_target="tpu_custom_call" | custom-call | flops 4000000000 | bytes 4000000 | tf_op jit(solution)/shard_map/pallas_call | solution.py:741
  48.3 0.0 collective-permute-done.in0
  48.3 0.0 collective-permute-done.1.in1
  48.3 0.0 collective-permute-done.2.in2
  48.3 0.0 collective-permute-done.3.in3
  48.3 6.6 %shard_map.187 = (f32[144,128]{1,0:T(8,128)S(1)}, f32[144,128]{1,0:T(8,128)S(1)}, f32[144,128]{1,0:T(8,128)S(1)}, f32[144,128]{1,0:T(8,128)S(1)}, f32[2,9,40,256...) custom-call(f32[8,128]{1,0:T(8,128)S(1)} %get-tuple-element.54.least, ...), custom_call_target="tpu_custom_call" | custom-call | flops 8000000000 | bytes 4000000 | tf_op jit(solution)/shard_map/pallas_call | solution.py:741
  55.0 0.1 collective-permute-start.4
  55.1 2.1 %collective-permute-start.5 = (f32[144,128]{1,0:T(8,128)S(1)}, f32[144,128]{1,0:T(8,128)S(1)}, u32[]{:S(2)}, u32[]{:S(2)}) collective-permute-start(f32[144,128]{1,0:T(8,128)S(1)} %get-tuple-element.85), channel_id=1, source_target_pairs={{0,1},{1,2},{2,3},{3,4},{4,5},{5,6},{6,7},{7,8},{8,9},{9,10},{10,1... | collective-permute-start | bytes 221192 | tf_op jit(solution)/shard_map/ppermute | solution.py:761
  57.1 0.3 collective-permute-start.6
  57.4 6.8 %collective-permute-start.7 = (f32[144,128]{1,0:T(8,128)S(1)}, f32[144,128]{1,0:T(8,128)S(1)}, u32[]{:S(2)}, u32[]{:S(2)}) collective-permute-start(f32[144,128]{1,0:T(8,128)S(1)} %get-tuple-element.87), channel_id=1, source_target_pairs={{0,254},{1,255},{2,0},{3,1},{4,2},{5,3},{6,4},{7,5},{8,6},{9,7},{1... | collective-permute-start | bytes 221192 | tf_op jit(solution)/shard_map/ppermute | solution.py:761
  64.3 3.8 %shard_map.188 = (f32[2,9,40,256]{3,2,1,0:T(8,128)S(1)}, f32[2,9,64,256]{3,2,1,0:T(8,128)S(1)}, f32[2,4,144,256]{3,2,1,0:T(8,128)S(1)}) custom-call(bf16[2,9,144,256]{3,2,1,0:T(8,128)(2,1)S(1)} %get-tuple-element.88.x3, f32[9,9,3,256]{3,2,1,0:T(4,128)S(1)} %get-tuple-element.58.star, f32[2,9,64,256]{3,2,1,0:T(8,128)S(1)} %get-tuple-element.89.faces, ...), custom_call_target="tpu_custom_call" | custom-call | flops 4000000000 | bytes 4000000 | tf_op jit(solution)/shard_map/pallas_call | solution.py:741
  68.1 0.0 collective-permute-done.4.in0
  68.1 0.0 collective-permute-done.5.in1
  68.1 0.0 collective-permute-done.6.in2
  68.1 0.0 collective-permute-done.7.in3
  68.1 3.4 %shard_map.189 = (f32[9,35,256]{2,1,0:T(8,128)}, f32[9,35,256]{2,1,0:T(8,128)}, f32[1,256]{1,0:T(1,128)}) custom-call(f32[144,128]{1,0:T(8,128)S(1)} %collective-permute-done.4.in0, f32[144,128]{1,0:T(8,128)S(1)} %collective-permute-done.5.in1, f32[144,128]{1,0:T(8,128)S(1)} %collective-permute-done.6.in2, f32[144,128]{1,0:T(8,128)S(1)} %collective-permute-done.7.in3, ...), custom_call_target="tpu_custom_call" | custom-call | flops 4000000000 | bytes 4000000 | tf_op jit(solution)/shard_map/pallas_call | solution.py:741
Async XLA Ops:
  2.1 30.9 %all-to-all-start = ((f32[256,1,256]{2,1,0:T(1,128)}), f32[256,1,256]{2,1,0:T(1,128)S(1)}, u32[]{:S(2)}, u32[]{:S(2)}) async-start(f32[256,1,256]{2,1,0:T(1,128)} %broadcast_in_dim.3), calls=%async_computation | async-start | bytes 524288 | tf_op jit(solution)/shard_map/all_to_all | solution.py:785
  33.1 11.2 %copy-start = (bf16[1024,1024]{1,0:T(8,128)(2,1)S(1)}, bf16[1024,1024]{1,0:T(8,128)(2,1)}, u32[]{:S(2)}) copy-start(bf16[1024,1024]{1,0:T(8,128)(2,1)} %get-tuple-element.62.pick_local) | copy-start | bytes 6291460
  36.0 12.3 %collective-permute-start = (f32[144,128]{1,0:T(8,128)S(1)}, f32[144,128]{1,0:T(8,128)S(1)}, u32[]{:S(2)}, u32[]{:S(2)}) collective-permute-start(f32[144,128]{1,0:T(8,128)S(1)} %get-tuple-element.66), channel_id=1, source_target_pairs={{0,2},{1,3},{2,4},{3,5},{4,6},{5,7},{6,8},{7,9},{8,10},{9,11},{10,... | collective-permute-start | bytes 221192 | tf_op jit(solution)/shard_map/ppermute | solution.py:761
  36.3 12.1 %collective-permute-start.1 = (f32[144,128]{1,0:T(8,128)S(1)}, f32[144,128]{1,0:T(8,128)S(1)}, u32[]{:S(2)}, u32[]{:S(2)}) collective-permute-start(f32[144,128]{1,0:T(8,128)S(1)} %get-tuple-element.67), channel_id=1, source_target_pairs={{0,1},{1,2},{2,3},{3,4},{4,5},{5,6},{6,7},{7,8},{8,9},{9,10},{10,1... | collective-permute-start | bytes 221192 | tf_op jit(solution)/shard_map/ppermute | solution.py:761
  37.5 10.8 %collective-permute-start.2 = (f32[144,128]{1,0:T(8,128)S(1)}, f32[144,128]{1,0:T(8,128)S(1)}, u32[]{:S(2)}, u32[]{:S(2)}) collective-permute-start(f32[144,128]{1,0:T(8,128)S(1)} %get-tuple-element.68), channel_id=1, source_target_pairs={{0,255},{1,0},{2,1},{3,2},{4,3},{5,4},{6,5},{7,6},{8,7},{9,8},{10,... | collective-permute-start | bytes 221192 | tf_op jit(solution)/shard_map/ppermute | solution.py:761
  37.5 10.8 %collective-permute-start.3 = (f32[144,128]{1,0:T(8,128)S(1)}, f32[144,128]{1,0:T(8,128)S(1)}, u32[]{:S(2)}, u32[]{:S(2)}) collective-permute-start(f32[144,128]{1,0:T(8,128)S(1)} %get-tuple-element.69), channel_id=1, source_target_pairs={{0,254},{1,255},{2,0},{3,1},{4,2},{5,3},{6,4},{7,5},{8,6},{9,7},{1... | collective-permute-start | bytes 221192 | tf_op jit(solution)/shard_map/ppermute | solution.py:761
  55.0 13.1 %collective-permute-start.4 = (f32[144,128]{1,0:T(8,128)S(1)}, f32[144,128]{1,0:T(8,128)S(1)}, u32[]{:S(2)}, u32[]{:S(2)}) collective-permute-start(f32[144,128]{1,0:T(8,128)S(1)} %get-tuple-element.84), channel_id=1, source_target_pairs={{0,2},{1,3},{2,4},{3,5},{4,6},{5,7},{6,8},{7,9},{8,10},{9,11},{10,... | collective-permute-start | bytes 221192 | tf_op jit(solution)/shard_map/ppermute | solution.py:761
  55.1 13.0 %collective-permute-start.5 = (f32[144,128]{1,0:T(8,128)S(1)}, f32[144,128]{1,0:T(8,128)S(1)}, u32[]{:S(2)}, u32[]{:S(2)}) collective-permute-start(f32[144,128]{1,0:T(8,128)S(1)} %get-tuple-element.85), channel_id=1, source_target_pairs={{0,1},{1,2},{2,3},{3,4},{4,5},{5,6},{6,7},{7,8},{8,9},{9,10},{10,1... | collective-permute-start | bytes 221192 | tf_op jit(solution)/shard_map/ppermute | solution.py:761
  57.1 10.9 %collective-permute-start.6 = (f32[144,128]{1,0:T(8,128)S(1)}, f32[144,128]{1,0:T(8,128)S(1)}, u32[]{:S(2)}, u32[]{:S(2)}) collective-permute-start(f32[144,128]{1,0:T(8,128)S(1)} %get-tuple-element.86), channel_id=1, source_target_pairs={{0,255},{1,0},{2,1},{3,2},{4,3},{5,4},{6,5},{7,6},{8,7},{9,8},{10,... | collective-permute-start | bytes 221192 | tf_op jit(solution)/shard_map/ppermute | solution.py:761
  57.4 10.6 %collective-permute-start.7 = (f32[144,128]{1,0:T(8,128)S(1)}, f32[144,128]{1,0:T(8,128)S(1)}, u32[]{:S(2)}, u32[]{:S(2)}) collective-permute-start(f32[144,128]{1,0:T(8,128)S(1)} %get-tuple-element.87), channel_id=1, source_target_pairs={{0,254},{1,255},{2,0},{3,1},{4,2},{5,3},{6,4},{7,5},{8,6},{9,7},{1... | collective-permute-start | bytes 221192 | tf_op jit(solution)/shard_map/ppermute | solution.py:761

commit v2 on v1

--- a/solution.py
+++ b/solution.py
@@ -33,62 +33,39 @@
     return hi, (x - hi.astype(F32)).astype(BF16)
 
 
-def place(mat, cols, hi_at, lo_at):
-    rows = mat.shape[1]
+def spread_columns(rows, cols, starts):
     gap = lax.broadcasted_iota(jnp.int32, (rows, cols), 1) - lax.broadcasted_iota(
         jnp.int32, (rows, cols), 0
     )
-
-    def ones(starts):
-        mask = gap == starts[0]
-        for start in starts[1:]:
-            mask = mask | (gap == start)
-        return jnp.where(mask, 1.0, 0.0).astype(BF16)
-
-    hi, lo = split(mat)
-    return dot(hi, ones(hi_at)) + dot(lo, ones(lo_at))
-
-
-def fill_stiff(out, stage, stiffness, transposed):
+    mask = gap == starts[0]
+    for start in starts[1:]:
+        mask = mask | (gap == start)
+    return jnp.where(mask, 1.0, 0.0).astype(BF16)
+
+
+def fill(out, stage, mats, step, period):
+    rows, cols = out.shape
     stage[...] = jnp.zeros(stage.shape, F32)
-    for d in range(3):
-        mat = stiffness[d]
-        if transposed:
-            mat = mat.T
-        stage[d * ROWS : d * ROWS + BASIS, 0 : 3 * PACK] = place(
-            mat, 3 * PACK, (0, PACK), (2 * PACK,)
-        )
-    out[...] = stage[0 : 3 * ROWS, 0 : 3 * PACK].astype(BF16)
-
-
-def fill_proj(out, stage, face_proj):
-    stage[...] = jnp.zeros(stage.shape, F32)
+    for k, mat in enumerate(mats):
+        stage[k * step : k * step + mat.shape[0], 0 : mat.shape[1]] = mat
+    hi, lo = split(stage[0:rows, :])
+    width = stage.shape[1]
+    out[...] = (
+        dot(hi, spread_columns(width, cols, (0, period)))
+        + dot(lo, spread_columns(width, cols, (2 * period,)))
+    ).astype(BF16)
+
+
+def fill_lift(out, face_lift):
+    total = None
     for f in range(4):
-        stage[f * FROWS : f * FROWS + FACE_BASIS, 0 : 3 * PACK] = place(
-            face_proj[:, f, :], 3 * PACK, (0, PACK), (2 * PACK,)
-        )
-    out[...] = stage[0 : 4 * FROWS, 0 : 3 * PACK].astype(BF16)
-
-
-def fill_orient(out, stage, face_orient):
-    stage[...] = jnp.zeros(stage.shape, F32)
-    for o in range(3):
-        stage[o * FROWS : o * FROWS + FACE_BASIS, 0 : 3 * FROWS] = place(
-            face_orient[o], 3 * FROWS, (0, FROWS), (2 * FROWS,)
-        )
-    out[...] = stage[0 : 3 * FROWS, 0 : 3 * FROWS].astype(BF16)
-
-
-def fill_lift(out, stage, face_lift):
-    stage[...] = jnp.zeros(stage.shape, F32)
-    total = jnp.zeros((BASIS, 12 * FROWS), F32)
-    for f in range(4):
+        hi, lo = split(face_lift[:, f, :].T)
         base = f * FROWS
-        total = total + place(
-            face_lift[:, f, :].T, 12 * FROWS, (base, 4 * FROWS + base), (8 * FROWS + base,)
-        )
-    stage[0:BASIS, 0 : 12 * FROWS] = total
-    out[...] = stage[0:ROWS, 0 : 12 * FROWS].astype(BF16)
+        part = dot(
+            hi, spread_columns(FACE_BASIS, 12 * FROWS, (base, 4 * FROWS + base))
+        ) + dot(lo, spread_columns(FACE_BASIS, 12 * FROWS, (8 * FROWS + base,)))
+        total = part if total is None else total + part
+    out[...] = jnp.concatenate([total, jnp.zeros((ROWS - BASIS, 12 * FROWS), F32)], 0).astype(BF16)
 
 
 def stack_split(x3, q, x):
@@ -191,8 +168,8 @@
     face_lift,
     face_orient,
     flux_local,
-    flux_neighbor,
     derived,
+    last,
     pick_local,
     pick_remote,
     pick_send,
@@ -206,7 +183,6 @@
     worient,
     star_kept,
     local_kept,
-    neighbor_kept,
     kind_kept,
     turn_kept,
     cluster_kept,
@@ -217,12 +193,14 @@
     series,
     raw,
     local_picks,
+    star_rows,
+    found,
     sems,
 ):
     copies = [
         pltpu.make_async_copy(source, kept, sems.at[2, i])
         for i, (source, kept) in enumerate(
-            ((star, star_kept), (flux_local, local_kept), (flux_neighbor, neighbor_kept))
+            ((star, star_kept), (flux_local, local_kept))
         )
     ]
     loads = [
@@ -234,11 +212,11 @@
     kind_kept[...] = face_kind[...]
     turn_kept[...] = orientation[...]
     cluster_kept[...] = cluster[...]
-    fill_stiff(wstiff, stage, stiffness, False)
-    fill_stiff(wstiff_t, stage, stiffness, True)
-    fill_proj(wproj, stage, face_proj)
-    fill_lift(wlift, stage, face_lift)
-    fill_orient(worient, stage, face_orient)
+    fill(wstiff, stage.at[0], [stiffness[d] for d in range(3)], ROWS, PACK)
+    fill(wstiff_t, stage.at[1], [stiffness[d].T for d in range(3)], ROWS, PACK)
+    fill(wproj, stage.at[2], [face_proj[:, f, :] for f in range(4)], FROWS, PACK)
+    fill(worient, stage.at[3], [face_orient[o] for o in range(3)], FROWS, FROWS)
+    fill_lift(wlift, face_lift)
 
     send_code = send_face[...] * ELEMS + send_element[...]
     for g in range(4):
@@ -269,24 +247,27 @@
     slot = lax.broadcasted_iota(jnp.int32, (HALF, ELEMS), 0)
     slot = jnp.where(slot < SLOTS, slot, slot - SLOTS)
     chosen = jnp.where(slot == place_of, 1.0, 0.0)
-    pick_t = chosen.T.astype(BF16)
     below = lax.broadcasted_iota(jnp.int32, (HALF, ELEMS), 0) < SLOTS
     for n in range(2):
         own = jnp.where(below, chosen, 0.0) if n == 0 else jnp.where(below, 0.0, chosen)
         give_fine[n] = own.astype(BF16)
         take_fine[n] = own.T.astype(BF16)
-    low1 = lax.broadcasted_iota(jnp.int32, (1, HALF), 1) < SLOTS
     copies[0].wait()
-    for d in range(3):
-        plain = []
-        for q in range(QUANT):
-            hi, lo = split(star[q, :, d, :])
-            plain.append(dot(hi, pick_t) + dot(lo, pick_t))
-        for q in range(QUANT):
-            for p in range(QUANT):
-                fine_star[q, p, d : d + 1, :] = jnp.where(
-                    low1, plain[q][p : p + 1], plain[p][q : q + 1]
-                )
+    for q in range(QUANT):
+        for p in range(QUANT):
+            base = 4 * (q * QUANT + p)
+            star_rows[base : base + 3, :] = star[q, p]
+    hi, lo = split(star_rows[...])
+    take = chosen.T.astype(BF16)
+    found[...] = dot(hi, take) + dot(lo, take)
+    low1 = lax.broadcasted_iota(jnp.int32, (3, HALF), 1) < SLOTS
+    for q in range(QUANT):
+        for p in range(QUANT):
+            plain = 4 * (q * QUANT + p)
+            swapped = 4 * (p * QUANT + q)
+            fine_star[q, p] = jnp.where(
+                low1, found[plain : plain + 3, :], found[swapped : swapped + 3, :]
+            )
 
     for n in range(2):
         loads[n].wait()
@@ -294,7 +275,7 @@
             series[0, n, q, 0:BASIS, :] = raw[n, q]
             series[0, n, q, BASIS:ROWS, :] = jnp.zeros((ROWS - BASIS, ELEMS), F32)
 
-    def step(degree, _):
+    def step(degree, write):
         for n in range(2):
             for q in range(QUANT):
                 stack_split(x3, q, series[degree, n, q])
@@ -303,24 +284,34 @@
             for half in range(2):
 
                 def emit(q, lanes, value):
-                    series[degree + 1, n, q, :, lanes] = value
+                    write(n, q, lanes, value)
 
                 star_apply(spread, star, n == 1, half, emit)
+
+    def stored(degree, n):
+        return pltpu.make_async_copy(
+            series.at[degree + 1, n], derived.at[n, degree], sems.at[n, degree]
+        )
+
+    def early_step(degree, _):
+        def write(n, q, lanes, value):
+            series[degree + 1, n, q, :, lanes] = value
+
+        step(degree, write)
         for n in range(2):
-            pltpu.make_async_copy(
-                series.at[degree + 1, n], derived.at[n, degree], sems.at[n, degree]
-            ).start()
+            stored(degree, n).start()
         return 0
 
-    lax.fori_loop(0, ORDER - 1, step, 0)
+    def write_last(n, q, lanes, value):
+        last[n, q, :, lanes] = value
+
+    lax.fori_loop(0, ORDER - 2, early_step, 0)
+    step(ORDER - 2, write_last)
     copies[1].wait()
-    copies[2].wait()
     table_out.wait()
     for n in range(2):
-        for degree in range(ORDER - 1):
-            pltpu.make_async_copy(
-                series.at[degree + 1, n], derived.at[n, degree], sems.at[n, degree]
-            ).wait()
+        for degree in range(ORDER - 2):
+            stored(degree, n).wait()
 
 
 def weights_of(smallest):
@@ -341,8 +332,10 @@
     fwd,
     adj,
     derived,
+    last,
     pick_send,
     wproj,
+    flux_neighbor,
     out0,
     out1,
     out2,
@@ -354,6 +347,7 @@
     series,
     start,
     least,
+    neighbor_kept,
     sems,
 ):
     outs = (out0, out1, out2, out3)
@@ -372,6 +366,8 @@
                 )
             )
             copies[n][part].start()
+    keeping = pltpu.make_async_copy(flux_neighbor, neighbor_kept, sems.at[2, 0])
+    keeping.start()
     smallest = jnp.min(steps[...])
     least[...] = jnp.full(least.shape, smallest, F32)
     early, _ = weights_of(smallest)
@@ -382,8 +378,8 @@
                 copies[n][q // third].wait()
             integral[n, q, 0:BASIS, :] = early[0] * start[n, q]
             integral[n, q, BASIS:ROWS, :] = jnp.zeros((ROWS - BASIS, ELEMS), F32)
-            total = integral[n, q]
-            for degree in range(1, ORDER):
+            total = integral[n, q] + early[ORDER - 1] * last[n, q]
+            for degree in range(1, ORDER - 1):
                 total = total + early[degree] * series[n, degree - 1, q]
             integral[n, q] = total
             stack_split(x3.at[n], q, total)
@@ -393,6 +389,7 @@
         outs[g][...] = value
 
     pack_send(table, pick_send, send)
+    keeping.wait()
 
 
 def flux_apply(source, weights, adjoint, n, f, half, acc):
@@ -647,6 +644,7 @@
     least,
     start,
     series,
+    last,
     volume,
     flux_sum,
     gathered,
@@ -661,8 +659,8 @@
         for q in range(QUANT):
             later[n, q, 0:BASIS, :] = late[0] * start[n, q]
             later[n, q, BASIS:ROWS, :] = jnp.zeros((ROWS - BASIS, ELEMS), F32)
-            total = later[n, q]
-            for degree in range(1, ORDER):
+            total = later[n, q] + late[ORDER - 1] * last[n, q]
+            for degree in range(1, ORDER - 1):
                 total = total + late[degree] * series[n, degree - 1, q]
             later[n, q] = total
 
@@ -782,7 +780,8 @@
     face_orient,
 ):
     count = lax.axis_size("dom")
-    steps = lax.all_to_all(jnp.broadcast_to(timescale, (count, 1, ELEMS)), "dom", 0, 0)
+    halves = jnp.minimum(timescale[:HALF], timescale[HALF:])
+    steps = lax.all_to_all(jnp.broadcast_to(halves, (count, 1, HALF)), "dom", 0, 0)
     cluster = cluster.reshape(1, ELEMS)
 
     fwd_dofs = jnp.transpose(fwd_dofs, (1, 0, 2))
@@ -801,7 +800,7 @@
     table_data = keep(4 * TABLE, 4 * ELEMS, **bf16)
     stacked = keep(2, QUANT, 3 * PACK, ELEMS, **bf16)
     fields = keep(2, QUANT, ROWS, ELEMS)
-    apart = (2, ORDER - 1, QUANT, ROWS, ELEMS)
+    apart = (2, ORDER - 2, QUANT, ROWS, ELEMS)
     spread = keep(QUANT, 3 * ROWS, ELEMS)
     remote_scratch = (
         keep(4 * TABLE, ELEMS, **bf16),
@@ -812,6 +811,7 @@
 
     (
         derived,
+        last,
         pick_local,
         pick_remote,
         pick_send,
@@ -825,7 +825,6 @@
         worient,
         star,
         flux_local,
-        flux_neighbor,
         face_kind,
         orientation,
         cluster,
@@ -847,10 +846,10 @@
             face_lift,
             face_orient,
             flux_local,
-            flux_neighbor,
         ),
         (
             pltpu.HBM(apart, F32),
+            fields,
             pltpu.HBM((4 * ELEMS, 4 * ELEMS), BF16),
             keep(ELEMS, 4 * ELEMS, **bf16),
             keep(4 * ELEMS, ELEMS, **bf16),
@@ -864,31 +863,32 @@
             keep(3 * FROWS, 3 * FROWS, **bf16),
             keep(*star.shape),
             keep(*flux_local.shape),
-            keep(*flux_neighbor.shape),
             keep(4, ELEMS, dtype=jnp.int32),
             keep(4, ELEMS, dtype=jnp.int32),
             keep(1, ELEMS, dtype=jnp.int32),
         ),
         (
-            keep(128, 256),
+            keep(4, 128, 128),
             keep(QUANT, 3 * PACK, ELEMS, **bf16),
             spread,
             keep(8, ELEMS, dtype=jnp.int32),
-            keep(ORDER, 2, QUANT, ROWS, ELEMS),
+            keep(ORDER - 1, 2, QUANT, ROWS, ELEMS),
             keep(2, QUANT, BASIS, ELEMS),
             keep(4 * ELEMS, 4 * ELEMS, **bf16),
+            keep(336, ELEMS),
+            keep(336, HALF),
             pltpu.SemaphoreType.DMA((4, ORDER - 1)),
         ),
         14000000000,
-        far=range(16),
-        spaces={0: away, 1: away, 2: away, 14: away, 15: away},
-        out_spaces={0: away, 1: away},
+        far=range(15),
+        spaces={0: away, 1: away, 2: away, 14: away},
+        out_spaces={0: away, 2: away},
     )
 
     local_out = (fields, face_data, keep(2, 4, TABLE, ELEMS))
-    *outgoing, integral, faces, table, x3, series, start, least = call(
+    *outgoing, integral, faces, table, x3, series, start, least, flux_neighbor = call(
         integral_kernel,
-        (steps, fwd_dofs, adj_dofs, derived, pick_send, wproj),
+        (steps, fwd_dofs, adj_dofs, derived, last, pick_send, wproj, flux_neighbor),
         (message,) * 4
         + (
             fields,
@@ -898,16 +898,17 @@
             keep(*apart),
             keep(2, QUANT, BASIS, ELEMS),
             keep(8, HALF),
+            keep(*flux_neighbor.shape),
         ),
-        (pltpu.SemaphoreType.DMA((2, 4)),),
+        (pltpu.SemaphoreType.DMA((3, 4)),),
         2000000000,
-        spaces={1: away, 2: away, 3: away},
-        far=(1, 2, 3),
+        spaces={1: away, 2: away, 3: away, 7: away},
+        far=(1, 2, 3, 7),
     )
     received = deliver(outgoing)
     volume, flux_sum, gathered, later = call(
         first_local_kernel,
-        (x3, star, faces, table, flux_local, pick_local, wstiff_t, least, start, series),
+        (x3, star, faces, table, flux_local, pick_local, wstiff_t, least, start, series, last),
         local_out + (fields,),
         (spread,),
         4000000000,

time: 71.9 us -> 69.9 us (0.972)
  waiting for transfers between devices: 2.09 us -> 0.76 us
  Pallas kernels: 33.9 us -> 32.9 us
  local copies, waits for them, and re-layouts: 1.52 us -> 0.73 us
  other arithmetic: 0 us -> 0.76 us
    all_to_all x1, waiting for transfers between devices: 2.07 us -> 0.74 us  [shards(): lax.all_to_all(jnp.broadcast_to(halves, (count, 1, HALF)), 'dom', 0, 0)]
    pallas_call x6, Pallas kernels: 33.9 us -> 32.9 us  [call(): pl.pallas_call(kernel, out_shape=outs, in_specs=[spaces.get(i, whole) for...]
    broadcast_in_dim x1, local copies, waits for them, and re-layouts: 1.52 us -> 0.72 us  [shards(): jnp.broadcast_to(halves, (count, 1, HALF))]
    min x0 -> x1, other arithmetic: none -> 0.76 us  [shards(): halves = jnp.minimum(timescale[:HALF], timescale[HALF:])]
where the time goes in v2:
time: 69.9 us; the launch traced here: 69.7 us
  starting transfers between devices  33.6 us (48%)
  Pallas kernels  32.9 us (47%)
  between operations  0.93 us (1%)
  other arithmetic  0.76 us (1%)
  waiting for transfers between devices  0.76 us (1%)
  local copies, waits for them, and re-layouts  0.73 us (1%)
    pallas_call x6, Pallas kernels, call(): pl.pallas_call(kernel, out_shape=outs, in_specs=[spaces.get(i, whole) for...  32.9 us
    ppermute x8, starting transfers between devices, deliver(): received.append(lax.ppermute(value, 'dom', pairs))  17.9 us
    all_to_all x1, starting transfers between devices, shards(): lax.all_to_all(jnp.broadcast_to(halves, (count, 1, HALF)), 'dom', 0, 0)  15.7 us
  transfers between devices with their start and end apart: 9, of which 1 were waited for; matrix products, arithmetic and copies ran while one was open for 0% of the time, Pallas kernels for 29%

profile of v2, /device:TPU:1, one launch (start us, length us, event | category | flops | bytes accessed | tf_op | source)
XLA Modules:
  0.0 69.7 jit_solution(7419436986148326049)
XLA Ops:
  0.6 0.8 %slice_minimum_fusion = f32[128]{0:T(128)S(1)} fusion(f32[256]{0:T(256)} %param.22), kind=kLoop, calls=%fused_computation | loop fusion | flops 128 | bytes 1536 | tf_op jit(solution)/shard_map/min | solution.py:783
  1.4 0.7 %broadcast_in_dim.3 = f32[256,1,128]{2,1,0:T(1,128)} broadcast(f32[128]{0:T(128)S(1)} %slice_minimum_fusion), dimensions={2} | broadcast | bytes 131584 | tf_op jit(solution)/shard_map/broadcast_in_dim | solution.py:784
  2.1 15.7 %all-to-all-start = ((f32[256,1,128]{2,1,0:T(1,128)}), f32[256,1,128]{2,1,0:T(1,128)S(1)}, u32[]{:S(2)}, u32[]{:S(2)}) async-start(f32[256,1,128]{2,1,0:T(1,128)} %broadcast_in_dim.3), calls=%async_computation | async-start | bytes 262144 | tf_op jit(solution)/shard_map/all_to_all | solution.py:784
  17.8 12.2 %shard_map.184 = (f32[2,3,9,40,256]{4,3,2,1,0:T(8,128)}, f32[2,9,40,256]{3,2,1,0:T(8,128)S(1)}, bf16[1024,1024]{1,0:T(8,128)(2,1)}, bf16[256,1024]{1,0:T(8,128)(...) custom-call(f32[9,35,256]{2,1,0:T(8,128)} %bitcast.11, ...), custom_call_target="tpu_custom_call" | custom-call | flops 14000000000 | bytes 4000000 | tf_op jit(solution)/shard_map/pallas_call | solution.py:739
  30.0 0.7 %all-to-all-done.steps = f32[256,1,128]{2,1,0:T(1,128)S(1)} async-done(((f32[256,1,128]{2,1,0:T(1,128)}), f32[256,1,128]{2,1,0:T(1,128)S(1)}, u32[]{:S(2)}, u32[]{:S(2)}) %all-to-all-start) | async-done | bytes 131104 | tf_op jit(solution)/shard_map/all_to_all | solution.py:784
  30.7 0.0 copy-start
  30.7 2.8 %shard_map.185 = (f32[144,128]{1,0:T(8,128)S(1)}, f32[144,128]{1,0:T(8,128)S(1)}, f32[144,128]{1,0:T(8,128)S(1)}, f32[144,128]{1,0:T(8,128)S(1)}, f32[2,9,40,256...) custom-call(f32[256,1,128]{2,1,0:T(1,128)S(1)} %all-to-all-done.step, ...), custom_call_target="tpu_custom_call" | custom-call | flops 2000000000 | bytes 4000000 | tf_op jit(solution)/shard_map/pallas_call | solution.py:739
  33.5 0.7 %collective-permute-start = (f32[144,128]{1,0:T(8,128)S(1)}, f32[144,128]{1,0:T(8,128)S(1)}, u32[]{:S(2)}, u32[]{:S(2)}) collective-permute-start(f32[144,128]{1,0:T(8,128)S(1)} %get-tuple-element.68), channel_id=1, source_target_pairs={{0,2},{1,3},{2,4},{3,5},{4,6},{5,7},{6,8},{7,9},{8,10},{9,11},{10,... | collective-permute-start | bytes 221192 | tf_op jit(solution)/shard_map/ppermute | solution.py:759
  34.2 1.7 %collective-permute-start.1 = (f32[144,128]{1,0:T(8,128)S(1)}, f32[144,128]{1,0:T(8,128)S(1)}, u32[]{:S(2)}, u32[]{:S(2)}) collective-permute-start(f32[144,128]{1,0:T(8,128)S(1)} %get-tuple-element.69), channel_id=1, source_target_pairs={{0,1},{1,2},{2,3},{3,4},{4,5},{5,6},{6,7},{7,8},{8,9},{9,10},{10,1... | collective-permute-start | bytes 221192 | tf_op jit(solution)/shard_map/ppermute | solution.py:759
  35.9 0.0 collective-permute-start.2
  36.0 6.3 %collective-permute-start.3 = (f32[144,128]{1,0:T(8,128)S(1)}, f32[144,128]{1,0:T(8,128)S(1)}, u32[]{:S(2)}, u32[]{:S(2)}) collective-permute-start(f32[144,128]{1,0:T(8,128)S(1)} %get-tuple-element.71), channel_id=1, source_target_pairs={{0,254},{1,255},{2,0},{3,1},{4,2},{5,3},{6,4},{7,5},{8,6},{9,7},{1... | collective-permute-start | bytes 221192 | tf_op jit(solution)/shard_map/ppermute | solution.py:759
  42.3 0.0 copy-done
  42.3 4.1 %shard_map.186 = (f32[2,9,40,256]{3,2,1,0:T(8,128)S(1)}, f32[2,9,64,256]{3,2,1,0:T(8,128)S(1)}, f32[2,4,144,256]{3,2,1,0:T(8,128)S(1)}, f32[2,9,40,256]{3,2,1,0:T(8,128)S(1)}) custom-call(bf16[2,9,144,256]{3,2,1,0:T(8,128)(2,1)S(1)} %get-tuple-element.59.x3, f32[9,9,3,256]{3,2,1,0:T(4,128)S(1)} %get-tuple-element.60.star, ...), custom_call_target="tpu_custom_call" | custom-call | flops 4000000000 | bytes 4000000 | tf_op jit(solution)/shard_map/pallas_call | solution.py:739
  46.3 0.0 collective-permute-done.in0
  46.3 0.0 collective-permute-done.1.in1
  46.3 0.0 collective-permute-done.2.in2
  46.4 0.0 collective-permute-done.3.in3
  46.4 6.6 %shard_map.187 = (f32[144,128]{1,0:T(8,128)S(1)}, f32[144,128]{1,0:T(8,128)S(1)}, f32[144,128]{1,0:T(8,128)S(1)}, f32[144,128]{1,0:T(8,128)S(1)}, f32[2,9,40,256...) custom-call(f32[8,128]{1,0:T(8,128)S(1)} %get-tuple-element.56.least, ...), custom_call_target="tpu_custom_call" | custom-call | flops 8000000000 | bytes 4000000 | tf_op jit(solution)/shard_map/pallas_call | solution.py:739
  53.0 0.1 collective-permute-start.4
  53.1 1.7 %collective-permute-start.5 = (f32[144,128]{1,0:T(8,128)S(1)}, f32[144,128]{1,0:T(8,128)S(1)}, u32[]{:S(2)}, u32[]{:S(2)}) collective-permute-start(f32[144,128]{1,0:T(8,128)S(1)} %get-tuple-element.87), channel_id=1, source_target_pairs={{0,1},{1,2},{2,3},{3,4},{4,5},{5,6},{6,7},{7,8},{8,9},{9,10},{10,1... | collective-permute-start | bytes 221192 | tf_op jit(solution)/shard_map/ppermute | solution.py:759
  54.8 0.4 collective-permute-start.6
  55.2 7.0 %collective-permute-start.7 = (f32[144,128]{1,0:T(8,128)S(1)}, f32[144,128]{1,0:T(8,128)S(1)}, u32[]{:S(2)}, u32[]{:S(2)}) collective-permute-start(f32[144,128]{1,0:T(8,128)S(1)} %get-tuple-element.89), channel_id=1, source_target_pairs={{0,254},{1,255},{2,0},{3,1},{4,2},{5,3},{6,4},{7,5},{8,6},{9,7},{1... | collective-permute-start | bytes 221192 | tf_op jit(solution)/shard_map/ppermute | solution.py:759
  62.2 3.8 %shard_map.188 = (f32[2,9,40,256]{3,2,1,0:T(8,128)S(1)}, f32[2,9,64,256]{3,2,1,0:T(8,128)S(1)}, f32[2,4,144,256]{3,2,1,0:T(8,128)S(1)}) custom-call(bf16[2,9,144,256]{3,2,1,0:T(8,128)(2,1)S(1)} %get-tuple-element.90.x3, f32[9,9,3,256]{3,2,1,0:T(4,128)S(1)} %get-tuple-element.60.star, f32[2,9,64,256]{3,2,1,0:T(8,128)S(1)} %get-tuple-element.91.faces, ...), custom_call_target="tpu_custom_call" | custom-call | flops 4000000000 | bytes 4000000 | tf_op jit(solution)/shard_map/pallas_call | solution.py:739
  66.0 0.0 collective-permute-done.4.in0
  66.0 0.0 collective-permute-done.5.in1
  66.0 0.0 collective-permute-done.6.in2
  66.0 0.0 collective-permute-done.7.in3
  66.0 3.5 %shard_map.189 = (f32[9,35,256]{2,1,0:T(8,128)}, f32[9,35,256]{2,1,0:T(8,128)}, f32[1,256]{1,0:T(1,128)}) custom-call(f32[144,128]{1,0:T(8,128)S(1)} %collective-permute-done.4.in0, f32[144,128]{1,0:T(8,128)S(1)} %collective-permute-done.5.in1, f32[144,128]{1,0:T(8,128)S(1)} %collective-permute-done.6.in2, f32[144,128]{1,0:T(8,128)S(1)} %collective-permute-done.7.in3, ...), custom_call_target="tpu_custom_call" | custom-call | flops 4000000000 | bytes 4000000 | tf_op jit(solution)/shard_map/pallas_call | solution.py:739
Async XLA Ops:
  2.1 28.6 %all-to-all-start = ((f32[256,1,128]{2,1,0:T(1,128)}), f32[256,1,128]{2,1,0:T(1,128)S(1)}, u32[]{:S(2)}, u32[]{:S(2)}) async-start(f32[256,1,128]{2,1,0:T(1,128)} %broadcast_in_dim.3), calls=%async_computation | async-start | bytes 262144 | tf_op jit(solution)/shard_map/all_to_all | solution.py:784
  30.7 11.6 %copy-start = (bf16[1024,1024]{1,0:T(8,128)(2,1)S(1)}, bf16[1024,1024]{1,0:T(8,128)(2,1)}, u32[]{:S(2)}) copy-start(bf16[1024,1024]{1,0:T(8,128)(2,1)} %get-tuple-element.64.pick_local) | copy-start | bytes 6291460
  33.5 12.8 %collective-permute-start = (f32[144,128]{1,0:T(8,128)S(1)}, f32[144,128]{1,0:T(8,128)S(1)}, u32[]{:S(2)}, u32[]{:S(2)}) collective-permute-start(f32[144,128]{1,0:T(8,128)S(1)} %get-tuple-element.68), channel_id=1, source_target_pairs={{0,2},{1,3},{2,4},{3,5},{4,6},{5,7},{6,8},{7,9},{8,10},{9,11},{10,... | collective-permute-start | bytes 221192 | tf_op jit(solution)/shard_map/ppermute | solution.py:759
  34.2 12.1 %collective-permute-start.1 = (f32[144,128]{1,0:T(8,128)S(1)}, f32[144,128]{1,0:T(8,128)S(1)}, u32[]{:S(2)}, u32[]{:S(2)}) collective-permute-start(f32[144,128]{1,0:T(8,128)S(1)} %get-tuple-element.69), channel_id=1, source_target_pairs={{0,1},{1,2},{2,3},{3,4},{4,5},{5,6},{6,7},{7,8},{8,9},{9,10},{10,1... | collective-permute-start | bytes 221192 | tf_op jit(solution)/shard_map/ppermute | solution.py:759
  35.9 10.4 %collective-permute-start.2 = (f32[144,128]{1,0:T(8,128)S(1)}, f32[144,128]{1,0:T(8,128)S(1)}, u32[]{:S(2)}, u32[]{:S(2)}) collective-permute-start(f32[144,128]{1,0:T(8,128)S(1)} %get-tuple-element.70), channel_id=1, source_target_pairs={{0,255},{1,0},{2,1},{3,2},{4,3},{5,4},{6,5},{7,6},{8,7},{9,8},{10,... | collective-permute-start | bytes 221192 | tf_op jit(solution)/shard_map/ppermute | solution.py:759
  36.0 10.4 %collective-permute-start.3 = (f32[144,128]{1,0:T(8,128)S(1)}, f32[144,128]{1,0:T(8,128)S(1)}, u32[]{:S(2)}, u32[]{:S(2)}) collective-permute-start(f32[144,128]{1,0:T(8,128)S(1)} %get-tuple-element.71), channel_id=1, source_target_pairs={{0,254},{1,255},{2,0},{3,1},{4,2},{5,3},{6,4},{7,5},{8,6},{9,7},{1... | collective-permute-start | bytes 221192 | tf_op jit(solution)/shard_map/ppermute | solution.py:759
  53.0 13.0 %collective-permute-start.4 = (f32[144,128]{1,0:T(8,128)S(1)}, f32[144,128]{1,0:T(8,128)S(1)}, u32[]{:S(2)}, u32[]{:S(2)}) collective-permute-start(f32[144,128]{1,0:T(8,128)S(1)} %get-tuple-element.86), channel_id=1, source_target_pairs={{0,2},{1,3},{2,4},{3,5},{4,6},{5,7},{6,8},{7,9},{8,10},{9,11},{10,... | collective-permute-start | bytes 221192 | tf_op jit(solution)/shard_map/ppermute | solution.py:759
  53.1 12.9 %collective-permute-start.5 = (f32[144,128]{1,0:T(8,128)S(1)}, f32[144,128]{1,0:T(8,128)S(1)}, u32[]{:S(2)}, u32[]{:S(2)}) collective-permute-start(f32[144,128]{1,0:T(8,128)S(1)} %get-tuple-element.87), channel_id=1, source_target_pairs={{0,1},{1,2},{2,3},{3,4},{4,5},{5,6},{6,7},{7,8},{8,9},{9,10},{10,1... | collective-permute-start | bytes 221192 | tf_op jit(solution)/shard_map/ppermute | solution.py:759
  54.8 11.2 %collective-permute-start.6 = (f32[144,128]{1,0:T(8,128)S(1)}, f32[144,128]{1,0:T(8,128)S(1)}, u32[]{:S(2)}, u32[]{:S(2)}) collective-permute-start(f32[144,128]{1,0:T(8,128)S(1)} %get-tuple-element.88), channel_id=1, source_target_pairs={{0,255},{1,0},{2,1},{3,2},{4,3},{5,4},{6,5},{7,6},{8,7},{9,8},{10,... | collective-permute-start | bytes 221192 | tf_op jit(solution)/shard_map/ppermute | solution.py:759
  55.2 10.9 %collective-permute-start.7 = (f32[144,128]{1,0:T(8,128)S(1)}, f32[144,128]{1,0:T(8,128)S(1)}, u32[]{:S(2)}, u32[]{:S(2)}) collective-permute-start(f32[144,128]{1,0:T(8,128)S(1)} %get-tuple-element.89), channel_id=1, source_target_pairs={{0,254},{1,255},{2,0},{3,1},{4,2},{5,3},{6,4},{7,5},{8,6},{9,7},{1... | collective-permute-start | bytes 221192 | tf_op jit(solution)/shard_map/ppermute | solution.py:759

commit v3 on v2

--- a/solution.py
+++ b/solution.py
@@ -150,6 +150,11 @@
 def one_hot(codes, first, rows):
     ids = lax.broadcasted_iota(jnp.int32, (rows, codes.shape[1]), 0) + first
     return jnp.where(ids == codes, 1.0, 0.0).astype(BF16)
+
+
+def least_kernel(timescale, halves):
+    least = jnp.minimum(timescale[:, 0:HALF], timescale[:, HALF:])
+    halves[...] = jnp.broadcast_to(least, halves.shape)
 
 
 def first_kernel(
@@ -463,8 +468,12 @@
         lanes = slice(f * ELEMS, f * ELEMS + ELEMS)
         rows = slice(f * FROWS, f * FROWS + FROWS)
         found = dot(rtable[...], pick_remote[:, lanes])
-        turn = orientation[f : f + 1, :]
-        surface = face_kind[f : f + 1, :] == 2
+        turn = jnp.broadcast_to(orientation[f : f + 1, :], (FROWS, ELEMS))
+        unturned = turn == 0
+        turned_once = turn == 1
+        mirror = jnp.broadcast_to(
+            jnp.where(face_kind[f : f + 1, :] == 2, 1.0, 0.0), (FROWS, ELEMS)
+        )
         for n in range(2):
             total = (
                 found[n * 2 * TABLE : n * 2 * TABLE + TABLE]
@@ -480,14 +489,12 @@
             for q in range(QUANT):
                 three = dot(worient[...], x3o[n, f, q])
                 turned = jnp.where(
-                    turn == 0,
+                    unturned,
                     three[0:FROWS],
-                    jnp.where(turn == 1, three[FROWS : 2 * FROWS], three[2 * FROWS : 3 * FROWS]),
+                    jnp.where(turned_once, three[FROWS : 2 * FROWS], three[2 * FROWS : 3 * FROWS]),
                 )
-                own = faces[n, q, rows, :]
-                if q in MIRRORED:
-                    own = -own
-                other[n, q, rows, :] = turned + jnp.where(surface, own, 0.0)
+                own = faces[n, q, rows, :] * mirror
+                other[n, q, rows, :] = turned - own if q in MIRRORED else turned + own
     for n in range(2):
         for f in range(4):
             rows = slice(f * FROWS, f * FROWS + FROWS)
@@ -551,8 +558,8 @@
     outs = (out0, out1, out2, out3)
     early, _ = weights_of(jnp.min(least[...]))
     x3c[QUANT // 2, :, HALF:] = jnp.zeros((3 * PACK, HALF), BF16)
-    fine = cluster[...] == 0
-    active = cluster[...] <= 1
+    fine = jnp.broadcast_to(cluster[...], (ROWS, ELEMS)) == 0
+    active = jnp.broadcast_to(cluster[...], (ROWS, ELEMS)) <= 1
 
     def emit_first(n, q, value):
         before = jnp.concatenate([start[n, q], jnp.zeros((ROWS - BASIS, ELEMS), F32)], 0)
@@ -693,7 +700,7 @@
     other,
     x3l,
 ):
-    active = cluster[...] <= 1
+    active = jnp.broadcast_to(cluster[...], (ROWS, ELEMS)) <= 1
     copies = [
         pltpu.make_async_copy(final.at[n], out, sems.at[n]) for n, out in enumerate((fwd, adj))
     ]
@@ -780,8 +787,15 @@
     face_orient,
 ):
     count = lax.axis_size("dom")
-    halves = jnp.minimum(timescale[:HALF], timescale[HALF:])
-    steps = lax.all_to_all(jnp.broadcast_to(halves, (count, 1, HALF)), "dom", 0, 0)
+    (halves,) = call(
+        least_kernel,
+        (timescale.reshape(1, ELEMS),),
+        (keep(count, HALF),),
+        (),
+        100000,
+        far=(0,),
+    )
+    steps = lax.all_to_all(halves.reshape(count, 1, HALF), "dom", 0, 0)
     cluster = cluster.reshape(1, ELEMS)
 
     fwd_dofs = jnp.transpose(fwd_dofs, (1, 0, 2))

time: 69.9 us -> 69.7 us (level)
  Pallas kernels: 32.9 us -> 34.2 us
  other arithmetic: 0.76 us -> 0 us
  local copies, waits for them, and re-layouts: 0.73 us -> 0.01 us
    pallas_call x6 -> x7, Pallas kernels: 32.9 us -> 34.2 us  [call(): pl.pallas_call(kernel, out_shape=outs, in_specs=[spaces.get(i, whole) for...]
    min x1 -> x0, other arithmetic: 0.76 us -> none  [shards(): halves = jnp.minimum(timescale[:HALF], timescale[HALF:])]
    broadcast_in_dim x1 -> x0, local copies, waits for them, and re-layouts: 0.72 us -> none  [shards(): jnp.broadcast_to(halves, (count, 1, HALF))]
where the time goes in v3:
time: 69.7 us; the launch traced here: 69.5 us
  Pallas kernels  34.2 us (49%)
  starting transfers between devices  33.6 us (48%)
  between operations  0.93 us (1%)
  waiting for transfers between devices  0.76 us (1%)
    pallas_call x7, Pallas kernels, call(): pl.pallas_call(kernel, out_shape=outs, in_specs=[spaces.get(i, whole) for...  34.2 us
    ppermute x8, starting transfers between devices, deliver(): received.append(lax.ppermute(value, 'dom', pairs))  18 us
    all_to_all x1, starting transfers between devices, shards(): steps = lax.all_to_all(halves.reshape(count, 1, HALF), 'dom', 0, 0)  15.7 us
  transfers between devices with their start and end apart: 9, of which 1 were waited for; matrix products, arithmetic and copies ran while one was open for 0% of the time, Pallas kernels for 29%

profile of v3, /device:TPU:1, one launch (start us, length us, event | category | flops | bytes accessed | tf_op | source)
XLA Modules:
  0.0 69.5 jit_solution(7553093981284934532)
XLA Ops:
  0.6 1.3 %shard_map.184 = f32[256,128]{1,0:T(8,128)} custom-call(f32[1,256]{1,0:T(1,128)} %bitcast.13), custom_call_target="tpu_custom_call" | custom-call | flops 100000 | bytes 4000000 | tf_op jit(solution)/shard_map/pallas_call | solution.py:746
  2.0 15.7 %all-to-all-start = ((f32[256,1,128]{2,1,0:T(1,128)}), f32[256,1,128]{2,1,0:T(1,128)S(1)}, u32[]{:S(2)}, u32[]{:S(2)}) async-start(f32[256,1,128]{2,1,0:T(1,128)} %bitcast.1), calls=%async_computation | async-start | bytes 262144 | tf_op jit(solution)/shard_map/all_to_all | solution.py:798
  17.6 12.2 %shard_map.185 = (f32[2,3,9,40,256]{4,3,2,1,0:T(8,128)}, f32[2,9,40,256]{3,2,1,0:T(8,128)S(1)}, bf16[1024,1024]{1,0:T(8,128)(2,1)}, bf16[256,1024]{1,0:T(8,128)(...) custom-call(f32[9,35,256]{2,1,0:T(8,128)} %bitcast.14, ...), custom_call_target="tpu_custom_call" | custom-call | flops 14000000000 | bytes 4000000 | tf_op jit(solution)/shard_map/pallas_call | solution.py:746
  29.8 0.7 %all-to-all-done.steps = f32[256,1,128]{2,1,0:T(1,128)S(1)} async-done(((f32[256,1,128]{2,1,0:T(1,128)}), f32[256,1,128]{2,1,0:T(1,128)S(1)}, u32[]{:S(2)}, u32[]{:S(2)}) %all-to-all-start) | async-done | bytes 131104 | tf_op jit(solution)/shard_map/all_to_all | solution.py:798
  30.6 0.0 copy-start
  30.6 2.8 %shard_map.186 = (f32[144,128]{1,0:T(8,128)S(1)}, f32[144,128]{1,0:T(8,128)S(1)}, f32[144,128]{1,0:T(8,128)S(1)}, f32[144,128]{1,0:T(8,128)S(1)}, f32[2,9,40,256...) custom-call(f32[256,1,128]{2,1,0:T(1,128)S(1)} %all-to-all-done.step, ...), custom_call_target="tpu_custom_call" | custom-call | flops 2000000000 | bytes 4000000 | tf_op jit(solution)/shard_map/pallas_call | solution.py:746
  33.3 0.8 %collective-permute-start = (f32[144,128]{1,0:T(8,128)S(1)}, f32[144,128]{1,0:T(8,128)S(1)}, u32[]{:S(2)}, u32[]{:S(2)}) collective-permute-start(f32[144,128]{1,0:T(8,128)S(1)} %get-tuple-element.68), channel_id=1, source_target_pairs={{0,2},{1,3},{2,4},{3,5},{4,6},{5,7},{6,8},{7,9},{8,10},{9,11},{10,... | collective-permute-start | bytes 221192 | tf_op jit(solution)/shard_map/ppermute | solution.py:766
  34.1 1.7 %collective-permute-start.1 = (f32[144,128]{1,0:T(8,128)S(1)}, f32[144,128]{1,0:T(8,128)S(1)}, u32[]{:S(2)}, u32[]{:S(2)}) collective-permute-start(f32[144,128]{1,0:T(8,128)S(1)} %get-tuple-element.69), channel_id=1, source_target_pairs={{0,1},{1,2},{2,3},{3,4},{4,5},{5,6},{6,7},{7,8},{8,9},{9,10},{10,1... | collective-permute-start | bytes 221192 | tf_op jit(solution)/shard_map/ppermute | solution.py:766
  35.8 0.0 collective-permute-start.2
  35.8 6.3 %collective-permute-start.3 = (f32[144,128]{1,0:T(8,128)S(1)}, f32[144,128]{1,0:T(8,128)S(1)}, u32[]{:S(2)}, u32[]{:S(2)}) collective-permute-start(f32[144,128]{1,0:T(8,128)S(1)} %get-tuple-element.71), channel_id=1, source_target_pairs={{0,254},{1,255},{2,0},{3,1},{4,2},{5,3},{6,4},{7,5},{8,6},{9,7},{1... | collective-permute-start | bytes 221192 | tf_op jit(solution)/shard_map/ppermute | solution.py:766
  42.1 0.0 copy-done
  42.1 4.1 %shard_map.187 = (f32[2,9,40,256]{3,2,1,0:T(8,128)S(1)}, f32[2,9,64,256]{3,2,1,0:T(8,128)S(1)}, f32[2,4,144,256]{3,2,1,0:T(8,128)S(1)}, f32[2,9,40,256]{3,2,1,0:T(8,128)S(1)}) custom-call(bf16[2,9,144,256]{3,2,1,0:T(8,128)(2,1)S(1)} %get-tuple-element.59.x3, f32[9,9,3,256]{3,2,1,0:T(4,128)S(1)} %get-tuple-element.60.star, ...), custom_call_target="tpu_custom_call" | custom-call | flops 4000000000 | bytes 4000000 | tf_op jit(solution)/shard_map/pallas_call | solution.py:746
  46.2 0.0 collective-permute-done.in0
  46.2 0.0 collective-permute-done.1.in1
  46.2 0.0 collective-permute-done.2.in2
  46.2 0.0 collective-permute-done.3.in3
  46.2 6.6 %shard_map.188 = (f32[144,128]{1,0:T(8,128)S(1)}, f32[144,128]{1,0:T(8,128)S(1)}, f32[144,128]{1,0:T(8,128)S(1)}, f32[144,128]{1,0:T(8,128)S(1)}, f32[2,9,40,256...) custom-call(f32[8,128]{1,0:T(8,128)S(1)} %get-tuple-element.56.least, ...), custom_call_target="tpu_custom_call" | custom-call | flops 8000000000 | bytes 4000000 | tf_op jit(solution)/shard_map/pallas_call | solution.py:746
  52.8 0.1 collective-permute-start.4
  52.9 1.7 %collective-permute-start.5 = (f32[144,128]{1,0:T(8,128)S(1)}, f32[144,128]{1,0:T(8,128)S(1)}, u32[]{:S(2)}, u32[]{:S(2)}) collective-permute-start(f32[144,128]{1,0:T(8,128)S(1)} %get-tuple-element.87), channel_id=1, source_target_pairs={{0,1},{1,2},{2,3},{3,4},{4,5},{5,6},{6,7},{7,8},{8,9},{9,10},{10,1... | collective-permute-start | bytes 221192 | tf_op jit(solution)/shard_map/ppermute | solution.py:766
  54.6 0.4 collective-permute-start.6
  55.0 7.0 %collective-permute-start.7 = (f32[144,128]{1,0:T(8,128)S(1)}, f32[144,128]{1,0:T(8,128)S(1)}, u32[]{:S(2)}, u32[]{:S(2)}) collective-permute-start(f32[144,128]{1,0:T(8,128)S(1)} %get-tuple-element.89), channel_id=1, source_target_pairs={{0,254},{1,255},{2,0},{3,1},{4,2},{5,3},{6,4},{7,5},{8,6},{9,7},{1... | collective-permute-start | bytes 221192 | tf_op jit(solution)/shard_map/ppermute | solution.py:766
  62.0 3.8 %shard_map.189 = (f32[2,9,40,256]{3,2,1,0:T(8,128)S(1)}, f32[2,9,64,256]{3,2,1,0:T(8,128)S(1)}, f32[2,4,144,256]{3,2,1,0:T(8,128)S(1)}) custom-call(bf16[2,9,144,256]{3,2,1,0:T(8,128)(2,1)S(1)} %get-tuple-element.90.x3, f32[9,9,3,256]{3,2,1,0:T(4,128)S(1)} %get-tuple-element.60.star, f32[2,9,64,256]{3,2,1,0:T(8,128)S(1)} %get-tuple-element.91.faces, ...), custom_call_target="tpu_custom_call" | custom-call | flops 4000000000 | bytes 4000000 | tf_op jit(solution)/shard_map/pallas_call | solution.py:746
  65.8 0.0 collective-permute-done.4.in0
  65.8 0.0 collective-permute-done.5.in1
  65.8 0.0 collective-permute-done.6.in2
  65.8 0.0 collective-permute-done.7.in3
  65.8 3.4 %shard_map.190 = (f32[9,35,256]{2,1,0:T(8,128)}, f32[9,35,256]{2,1,0:T(8,128)}, f32[1,256]{1,0:T(1,128)}) custom-call(f32[144,128]{1,0:T(8,128)S(1)} %collective-permute-done.4.in0, f32[144,128]{1,0:T(8,128)S(1)} %collective-permute-done.5.in1, f32[144,128]{1,0:T(8,128)S(1)} %collective-permute-done.6.in2, f32[144,128]{1,0:T(8,128)S(1)} %collective-permute-done.7.in3, ...), custom_call_target="tpu_custom_call" | custom-call | flops 4000000000 | bytes 4000000 | tf_op jit(solution)/shard_map/pallas_call | solution.py:746
Async XLA Ops:
  2.0 28.6 %all-to-all-start = ((f32[256,1,128]{2,1,0:T(1,128)}), f32[256,1,128]{2,1,0:T(1,128)S(1)}, u32[]{:S(2)}, u32[]{:S(2)}) async-start(f32[256,1,128]{2,1,0:T(1,128)} %bitcast.1), calls=%async_computation | async-start | bytes 262144 | tf_op jit(solution)/shard_map/all_to_all | solution.py:798
  30.6 11.6 %copy-start = (bf16[1024,1024]{1,0:T(8,128)(2,1)S(1)}, bf16[1024,1024]{1,0:T(8,128)(2,1)}, u32[]{:S(2)}) copy-start(bf16[1024,1024]{1,0:T(8,128)(2,1)} %get-tuple-element.64.pick_local) | copy-start | bytes 6291460
  33.3 12.8 %collective-permute-start = (f32[144,128]{1,0:T(8,128)S(1)}, f32[144,128]{1,0:T(8,128)S(1)}, u32[]{:S(2)}, u32[]{:S(2)}) collective-permute-start(f32[144,128]{1,0:T(8,128)S(1)} %get-tuple-element.68), channel_id=1, source_target_pairs={{0,2},{1,3},{2,4},{3,5},{4,6},{5,7},{6,8},{7,9},{8,10},{9,11},{10,... | collective-permute-start | bytes 221192 | tf_op jit(solution)/shard_map/ppermute | solution.py:766
  34.1 12.1 %collective-permute-start.1 = (f32[144,128]{1,0:T(8,128)S(1)}, f32[144,128]{1,0:T(8,128)S(1)}, u32[]{:S(2)}, u32[]{:S(2)}) collective-permute-start(f32[144,128]{1,0:T(8,128)S(1)} %get-tuple-element.69), channel_id=1, source_target_pairs={{0,1},{1,2},{2,3},{3,4},{4,5},{5,6},{6,7},{7,8},{8,9},{9,10},{10,1... | collective-permute-start | bytes 221192 | tf_op jit(solution)/shard_map/ppermute | solution.py:766
  35.8 10.4 %collective-permute-start.2 = (f32[144,128]{1,0:T(8,128)S(1)}, f32[144,128]{1,0:T(8,128)S(1)}, u32[]{:S(2)}, u32[]{:S(2)}) collective-permute-start(f32[144,128]{1,0:T(8,128)S(1)} %get-tuple-element.70), channel_id=1, source_target_pairs={{0,255},{1,0},{2,1},{3,2},{4,3},{5,4},{6,5},{7,6},{8,7},{9,8},{10,... | collective-permute-start | bytes 221192 | tf_op jit(solution)/shard_map/ppermute | solution.py:766
  35.8 10.4 %collective-permute-start.3 = (f32[144,128]{1,0:T(8,128)S(1)}, f32[144,128]{1,0:T(8,128)S(1)}, u32[]{:S(2)}, u32[]{:S(2)}) collective-permute-start(f32[144,128]{1,0:T(8,128)S(1)} %get-tuple-element.71), channel_id=1, source_target_pairs={{0,254},{1,255},{2,0},{3,1},{4,2},{5,3},{6,4},{7,5},{8,6},{9,7},{1... | collective-permute-start | bytes 221192 | tf_op jit(solution)/shard_map/ppermute | solution.py:766
  52.8 13.0 %collective-permute-start.4 = (f32[144,128]{1,0:T(8,128)S(1)}, f32[144,128]{1,0:T(8,128)S(1)}, u32[]{:S(2)}, u32[]{:S(2)}) collective-permute-start(f32[144,128]{1,0:T(8,128)S(1)} %get-tuple-element.86), channel_id=1, source_target_pairs={{0,2},{1,3},{2,4},{3,5},{4,6},{5,7},{6,8},{7,9},{8,10},{9,11},{10,... | collective-permute-start | bytes 221192 | tf_op jit(solution)/shard_map/ppermute | solution.py:766
  52.9 12.9 %collective-permute-start.5 = (f32[144,128]{1,0:T(8,128)S(1)}, f32[144,128]{1,0:T(8,128)S(1)}, u32[]{:S(2)}, u32[]{:S(2)}) collective-permute-start(f32[144,128]{1,0:T(8,128)S(1)} %get-tuple-element.87), channel_id=1, source_target_pairs={{0,1},{1,2},{2,3},{3,4},{4,5},{5,6},{6,7},{7,8},{8,9},{9,10},{10,1... | collective-permute-start | bytes 221192 | tf_op jit(solution)/shard_map/ppermute | solution.py:766
  54.6 11.2 %collective-permute-start.6 = (f32[144,128]{1,0:T(8,128)S(1)}, f32[144,128]{1,0:T(8,128)S(1)}, u32[]{:S(2)}, u32[]{:S(2)}) collective-permute-start(f32[144,128]{1,0:T(8,128)S(1)} %get-tuple-element.88), channel_id=1, source_target_pairs={{0,255},{1,0},{2,1},{3,2},{4,3},{5,4},{6,5},{7,6},{8,7},{9,8},{10,... | collective-permute-start | bytes 221192 | tf_op jit(solution)/shard_map/ppermute | solution.py:766
  55.0 10.9 %collective-permute-start.7 = (f32[144,128]{1,0:T(8,128)S(1)}, f32[144,128]{1,0:T(8,128)S(1)}, u32[]{:S(2)}, u32[]{:S(2)}) collective-permute-start(f32[144,128]{1,0:T(8,128)S(1)} %get-tuple-element.89), channel_id=1, source_target_pairs={{0,254},{1,255},{2,0},{3,1},{4,2},{5,3},{6,4},{7,5},{8,6},{9,7},{1... | collective-permute-start | bytes 221192 | tf_op jit(solution)/shard_map/ppermute | solution.py:766
